TPU v7x, 512 devices: a whole 4x8x8 slice. The times are simulated.
512 devices in a mesh: theta: 32 (over x_lo, z, core), gz: 16 (over y, x_hi).
Axes of the slice: x: 4 (x_hi: 2, x_lo: 2; x = x_hi * 2 + x_lo), y: 8, z: 8, core: 2. Of those that a mesh axis runs over, the one named last changes fastest.
Arguments:
- velocity: float32 [3, 256, 256, 256], P(None, 'theta', 'gz'), may hold values from -6 to 6
- adjoint_seed: float32 [3, 256, 256, 256], P(None, 'theta', 'gz'), may hold values from -6 to 6
- rotor_offset: int32 [2], replicated, may hold values from 0 to 255
- design_mask: int32 [256, 256, 256], P('theta', 'gz'), may hold values 0 or 1
- interface_band_weight: bfloat16 [256, 8], replicated, may hold values from -0.375 to 0.375
Outputs:
- ending_velocity: float32 [3, 256, 256, 256], P(None, 'theta', 'gz')
- adjoint_field: float32 [3, 256, 256, 256], P(None, 'theta', 'gz')
All inputs are finite; a program needn't handle non-finite values. No bound on the sum of `design_mask` on one device may be relied on, other than what follows from the above.
Results may differ from a plain program's by a relative error of at most 0.00076.
Values sent between devices are 32-bit elements; how exact they have to be, the bound alone decides.
No kernel may reach another device: no remote copies, remote signals or barrier semaphores. Data moves between devices by JAX's collectives and lax.ppermute only.
A program may use at most 64 MiB of HBM per device.

v0:
```python
import jax
import jax.numpy as jnp
from jax import lax
from jax.sharding import PartitionSpec as P

NR = 256
RB = 128
BAND = 8
STEPS = 2
LOWER = RB - BAND // 2
UPPER = RB + BAND // 2
ZH = 4


def shifted(x, axis, by):
    peers = lax.axis_size(axis)
    return lax.ppermute(x, axis, [(i, (i + by) % peers) for i in range(peers)])


def stepped(x, axis, by):
    peers = lax.axis_size(axis)
    return lax.ppermute(x, axis, [(i, i + by) for i in range(peers) if 0 <= i + by < peers])


def nearest(shift, width):
    half = width // 2
    return (shift + half) // width, (shift + half) % width - half


def to_block(rotor, blocks):
    peers = lax.axis_size("theta")
    moves = [lambda x, b=b: shifted(x, "theta", b) for b in range(peers)]
    return lax.switch(jnp.mod(blocks, peers), moves, rotor)


def exact(rotor, shift):
    peers = lax.axis_size("theta")
    width = rotor.shape[1]
    group = width // 2
    shift = jnp.mod(shift, width * peers)

    def move(total):
        blocks, rest = divmod(total * group, width)

        def run(x):
            here = shifted(x[:, : width - rest], "theta", blocks)
            before = shifted(x[:, width - rest - group + 1 :], "theta", blocks + 1)
            return jnp.concatenate([before, here], axis=1)

        return run

    rows = lax.switch(shift // group, [move(i) for i in range(peers * width // group)], rotor)
    return lax.dynamic_slice_in_dim(rows, group - 1 - shift % group, width, axis=1)


def widened(rotor, stator, remain, h, extra=None):
    width = rotor.shape[1]
    reach = width // 2 + h
    up = [rotor[:, width - reach :], stator[:, width - h :]]
    down = [rotor[:, :reach], stator[:, :h]]
    if extra is not None:
        up += [extra[:, -1:, :, :RB], extra[:, -1:, :, RB:]]
        down += [extra[:, :1, :, :RB], extra[:, :1, :, RB:]]
    low = shifted(jnp.concatenate(up, axis=1), "theta", 1)
    high = shifted(jnp.concatenate(down, axis=1), "theta", -1)
    rotors = jnp.concatenate([low[:, :reach], rotor, high[:, :reach]], axis=1)
    aligned = lax.dynamic_slice_in_dim(rotors, reach - h - remain, width + 2 * h, axis=1)
    stators = jnp.concatenate([low[:, reach : reach + h], stator, high[:, reach : reach + h]], axis=1)
    whole = jnp.concatenate([aligned, stators], axis=3)
    if extra is None:
        return whole
    before = jnp.concatenate([low[:, reach + h : reach + h + 1], low[:, reach + h + 1 :]], axis=3)
    after = jnp.concatenate([high[:, reach + h : reach + h + 1], high[:, reach + h + 1 :]], axis=3)
    return whole, jnp.concatenate([before, extra, after], axis=1)


def beside(x):
    mid = x[:, 1:-1]
    zpad = jnp.pad(mid, ((0, 0), (0, 0), (1, 1), (0, 0)))
    rpad = jnp.pad(mid, ((0, 0), (0, 0), (0, 0), (1, 1)))
    return mid, x[:, 2:], x[:, :-2], zpad[:, :, 2:], zpad[:, :, :-2], rpad[..., 2:], rpad[..., :-2]


def viscosity(w):
    _, tp, tm, zp, zm, rp, rm = beside(w)
    strain_rate = jnp.sum(
        ((tp - tm) * 0.5) ** 2 + ((zp - zm) * 0.5) ** 2 + ((rp - rm) * 0.5) ** 2, axis=0
    )
    return 0.05 + 0.95 * (1.0 + 4.0 * strain_rate) ** (-0.25)


def laplace(x):
    mid, tp, tm, zp, zm, rp, rm = beside(x)
    return tp + tm + zp + zm + rp + rm - 6.0 * mid


def mixed(v, spread):
    flat = v.astype(jnp.bfloat16).reshape(-1, NR)
    return v + jnp.dot(flat, spread, preferred_element_type=jnp.float32).reshape(v.shape)


def coupled(a, weight):
    band = a[..., LOWER:UPPER].astype(jnp.bfloat16).reshape(-1, BAND)
    return a + jnp.dot(band, weight.T, preferred_element_type=jnp.float32).reshape(a.shape)


def axial_halo(field, seed, solid):
    nz = field.shape[2]

    def packed(cut):
        layers = jnp.moveaxis(cut(solid, 3, 1), 1, 0)[:, :, None]
        return jnp.concatenate(
            [cut(field, ZH, 2), cut(seed, 2, 2), layers, jnp.zeros_like(layers)], axis=2
        )

    low = stepped(packed(lambda x, n, d: lax.slice_in_dim(x, nz - n, nz, axis=d)), "gz", 1)
    high = stepped(packed(lambda x, n, d: lax.slice_in_dim(x, 0, n, axis=d)), "gz", -1)

    def layers_of(x):
        return jnp.moveaxis(x[:, :, ZH + 2], 0, 1)

    none = jnp.zeros_like(seed[:, :, :2])
    blank = jnp.zeros_like(solid[:, :1])
    return (
        jnp.concatenate([low[:, :, :ZH], field, high[:, :, :ZH]], axis=2),
        jnp.concatenate([none, low[:, :, ZH : ZH + 2], seed, high[:, :, ZH : ZH + 2], none], axis=2),
        jnp.concatenate([blank, layers_of(low), solid, layers_of(high), blank], axis=1),
    )


def body(velocity, adjoint_seed, rotor_offset, design_mask, interface_band_weight):
    width, nz = velocity.shape[1], velocity.shape[2]
    solid = design_mask.astype(jnp.float32)
    spread = jnp.pad(interface_band_weight, ((0, 0), (LOWER, NR - UPPER)))
    blocks0, remain0 = nearest(rotor_offset[0], width)
    blocks1, remain1 = nearest(rotor_offset[1], width)
    back1, away1 = nearest(-rotor_offset[1], width)

    rotor = to_block(velocity[..., :RB], blocks0)
    field = jnp.concatenate([rotor, velocity[..., RB:]], axis=3)
    field, seed, solid = axial_halo(field, adjoint_seed, solid)
    layer = lax.axis_index("gz") * nz - ZH + lax.broadcasted_iota(jnp.int32, (nz + 2 * ZH, 1), 0)
    inside = ((layer >= 0) & (layer < nz * lax.axis_size("gz"))).astype(jnp.float32)

    moved, seed = widened(field[..., :RB], field[..., RB:], remain0, 2, seed)
    w = mixed(moved, spread)
    visc0 = viscosity(w)
    mid = w[:, 2:-2]
    u = inside * (mid + 0.1 * visc0[1:-1] * laplace(w[:, 1:-1]) - 0.5 * solid * mid)

    rotor = to_block(u[..., :RB], blocks1)
    w = mixed(widened(rotor, u[..., RB:], remain1, 2), spread)
    visc1 = viscosity(w)
    mid = w[:, 2:-2]
    ending = (mid + 0.1 * visc1[1:-1] * laplace(w[:, 1:-1]) - 0.5 * solid * mid)[:, :, ZH:-ZH]
    lam = seed[:, 1:-1]
    lam = inside * coupled(lam + 0.1 * laplace(visc1 * seed) - 0.5 * solid * lam, interface_band_weight)

    rotor = to_block(lam[..., :RB], back1)
    lam = widened(rotor, lam[..., RB:], away1, 1)
    scaled = laplace(visc0 * lam)[:, :, ZH:-ZH]
    lam = lam[:, 1:-1, ZH:-ZH]
    lam = coupled(lam + 0.1 * scaled - 0.5 * solid[:, ZH:-ZH] * lam, interface_band_weight)
    rotor = exact(lam[..., :RB], -rotor_offset[0])
    return ending, jnp.concatenate([rotor, lam[..., RB:]], axis=3)


def solution(mesh):
    return jax.shard_map(
        body,
        mesh=mesh,
        in_specs=(
            P(None, "theta", "gz", None),
            P(None, "theta", "gz", None),
            P(),
            P("theta", "gz", None),
            P(),
        ),
        out_specs=(P(None, "theta", "gz", None), P(None, "theta", "gz", None)),
        check_vma=False,
    )
```

profile of v0, /device:TPU:29, one launch (start us, length us, event | category | flops | bytes accessed | tf_op | source)
XLA Modules:
  0.0 129.1 jit_solution(5253148570152294564)
XLA Ops:
  0.6 1.3 %fusion.92 = (s32[1]{0:T(128)}, s32[1]{0:T(128)}) fusion(s32[2]{0:T(128)} %param.167), kind=kLoop, calls=%fused_computation.243 | loop fusion | bytes 16 | tf_op jit(solution)/shard_map/slice | solution.py:136
  2.6 1.1 fusion.87
  3.7 18.8 %conditional.4 = (f32[3,8,16,128]{3,1,0,2:T(8,128)S(1)}) conditional(s32[]{:T(128)} %clamp.13, f32[3,8,16,128]{3,2,1,0:T(8,128)S(1)} %get-tuple-element.424, f32[3,8,16,128]{3,2,1,0:T(8,128)S(1)} %get-tuple-element.424, f32[3,8,16,128]{3,2,1,0:T(8,128)S(1)} %get-tuple-element.424, ...), branch_computations={%region_0.1_spmd, %region_1.2_spmd, %region_2.3_spmd, %region_3.4_... | conditional | bytes 1179696 | solution.py:33
  3.8 11.9 %collective-permute-start.29 = (f32[3,8,16,128]{3,2,1,0:T(8,128)S(1)}, f32[3,8,16,128]{3,2,1,0:T(8,128)S(1)}, u32[]{:S(2)}, u32[]{:S(2)}) collective-permute-start(f32[3,8,16,128]{3,2,1,0:T(8,128)S(1)} %param.29), channel_id=1, source_target_pairs={{0,464},{16,480},{32,496},{48,0},{64,16},{80,32},{96,48},{112,64},... | collective-permute-start | bytes 589832 | tf_op jit(solution)/shard_map/cond/branch_29_fun/ppermute | solution.py:17
  15.6 6.8 %collective-permute-done.29 = f32[3,8,16,128]{3,2,1,0:T(8,128)S(1)} collective-permute-done((f32[3,8,16,128]{3,2,1,0:T(8,128)S(1)}, f32[3,8,16,128]{3,2,1,0:T(8,128)S(1)}, u32[]{:S(2)}, u32[]{:S(2)}) %collective-permute-start.29) | collective-permute-done | bytes 196640 | tf_op jit(solution)/shard_map/cond/branch_29_fun/ppermute | solution.py:17
  23.8 4.7 %collective-permute-start.224 = (f32[3,8,8,256]{3,1,0,2:T(8,128)S(1)}, f32[3,8,8,256]{3,1,0,2:T(8,128)S(1)}, u32[]{:S(2)}, u32[]{:S(2)}) collective-permute-start(f32[3,8,8,256]{3,1,0,2:T(8,128)S(1)} %maximum_maximum_fusion.3), channel_id=1, source_target_pairs={{0,1},{1,2},{2,3},{3,4},{4,5},{5,6},{6,7},{7,8},{8,9},{9,10},{10,1... | collective-permute-start | bytes 589832 | tf_op jit(solution)/shard_map/ppermute | solution.py:22
  28.6 2.1 %collective-permute-start.225 = (f32[3,8,8,256]{3,2,1,0:T(8,128)S(1)}, f32[3,8,8,256]{3,2,1,0:T(8,128)S(1)}, u32[]{:S(2)}, u32[]{:S(2)}) collective-permute-start(f32[3,8,8,256]{3,2,1,0:T(8,128)S(1)} %maximum_maximum_fusion.4), channel_id=1, source_target_pairs={{1,0},{2,1},{3,2},{4,3},{5,4},{6,5},{7,6},{8,7},{9,8},{10,9},{11,1... | collective-permute-start | bytes 589832 | tf_op jit(solution)/shard_map/ppermute | solution.py:22
  34.4 5.5 %collective-permute-done.225 = f32[3,8,8,256]{3,2,1,0:T(8,128)S(1)} collective-permute-done((f32[3,8,8,256]{3,2,1,0:T(8,128)S(1)}, f32[3,8,8,256]{3,2,1,0:T(8,128)S(1)}, u32[]{:S(2)}, u32[]{:S(2)}) %collective-permute-start.225) | collective-permute-done | bytes 196640 | tf_op jit(solution)/shard_map/ppermute | solution.py:22
  41.4 1.9 %collective-permute-start.226 = (f32[3,10,24,128]{3,2,1,0:T(8,128)S(1)}, f32[3,10,24,128]{3,2,1,0:T(8,128)S(1)}, u32[]{:S(2)}, u32[]{:S(2)}) collective-permute-start(f32[3,10,24,128]{3,2,1,0:T(8,128)S(1)} %get-tuple-element.409), channel_id=1, source_target_pairs={{0,16},{16,32},{32,48},{48,64},{64,80},{80,96},{96,112},{112,128},... | collective-permute-start | bytes 1105928 | tf_op jit(solution)/shard_map/ppermute | solution.py:17
  43.3 3.5 %collective-permute-start.227 = (f32[3,10,24,128]{3,2,1,0:T(8,128)S(1)}, f32[3,10,24,128]{3,2,1,0:T(8,128)S(1)}, u32[]{:S(2)}, u32[]{:S(2)}) collective-permute-start(f32[3,10,24,128]{3,2,1,0:T(8,128)S(1)} %get-tuple-element.410), channel_id=1, source_target_pairs={{0,496},{16,0},{32,16},{48,32},{64,48},{80,64},{96,80},{112,96},{1... | collective-permute-start | bytes 1105928 | tf_op jit(solution)/shard_map/ppermute | solution.py:17
  48.8 3.7 %collective-permute-done.227 = f32[3,10,24,128]{3,2,1,0:T(8,128)S(1)} collective-permute-done((f32[3,10,24,128]{3,2,1,0:T(8,128)S(1)}, f32[3,10,24,128]{3,2,1,0:T(8,128)S(1)}, u32[]{:S(2)}, u32[]{:S(2)}) %collective-permute-start.227) | collective-permute-done | bytes 368672 | tf_op jit(solution)/shard_map/ppermute | solution.py:17
  55.5 1.8 %fusion.31 = f32[3,8,24,256]{3,2,1,0:T(8,128)S(1)} fusion(f32[3,8,24,256]{3,2,1,0:T(8,128)S(1)} %slice-done, f32[3,12,24,256]{3,2,1,0:T(8,128)} %copy-done, f32[8,24,256]{2,1,0:T(8,128)S(1)} %copy.17, f32[8,24,256]{2,1,0:T(8,128)S(1)} %slice_multiply_fusion.2, f32[24]{0:T(128)S(1)} %and_convert_fusion), kind=kLoop, calls=%fused_computation.138 | loop fusion | flops 1769472 | bytes 2752608 | tf_op jit(solution)/shard_map/mul | solution.py:149
  57.3 12.8 %conditional.5 = (f32[3,8,24,128]{3,2,1,0:T(8,128)}) conditional(s32[]{:T(128)} %clamp.12, (f32[3,8,24,256]{3,2,1,0:T(8,128)S(1)}) %tuple.489, (f32[3,8,24,256]{3,2,1,0:T(8,128)S(1)}) %tuple.489, (f32[3,8,24,256]{3,2,1,0:T(8,128)S(1)}) %tuple.489, (f32[3,8,24,256]{3,2,1,0:T(8,128)S(1)}) %tuple.489, ...), branch_computations={%region_33.34_spmd, %region_34.35_spmd, %region_35.36_spmd, %regio... | conditional | bytes 1769520 | solution.py:33
  57.4 8.4 %collective-permute-start.46 = (f32[3,8,24,128]{3,2,1,0:T(8,128)S(1)}, f32[3,8,24,128]{3,2,1,0:T(8,128)}, u32[]{:S(2)}, u32[]{:S(2)}) collective-permute-start(f32[3,8,24,128]{3,2,1,0:T(8,128)S(1)} %slice.1224), channel_id=1, source_target_pairs={{0,224},{16,240},{32,256},{48,272},{64,288},{80,304},{96,320},{112... | collective-permute-start | bytes 884744 | tf_op jit(solution)/shard_map/cond/branch_14_fun/ppermute | solution.py:17
  65.8 4.3 %collective-permute-done.46 = f32[3,8,24,128]{3,2,1,0:T(8,128)} collective-permute-done((f32[3,8,24,128]{3,2,1,0:T(8,128)S(1)}, f32[3,8,24,128]{3,2,1,0:T(8,128)}, u32[]{:S(2)}, u32[]{:S(2)}) %collective-permute-start.46) | collective-permute-done | bytes 294944 | tf_op jit(solution)/shard_map/cond/branch_14_fun/ppermute | solution.py:17
  70.1 1.1 fusion.91
  71.2 1.9 %collective-permute-start.228 = (f32[3,8,24,128]{3,2,1,0:T(8,128)S(1)}, f32[3,8,24,128]{3,2,1,0:T(8,128)S(1)}, u32[]{:S(2)}, u32[]{:S(2)}) collective-permute-start(f32[3,8,24,128]{3,2,1,0:T(8,128)S(1)} %pad_maximum_fusion.66), channel_id=1, source_target_pairs={{0,16},{16,32},{32,48},{48,64},{64,80},{80,96},{96,112},{112,128},... | collective-permute-start | bytes 884744 | tf_op jit(solution)/shard_map/ppermute | solution.py:17
  73.2 2.4 %collective-permute-start.229 = (f32[3,8,24,128]{3,2,1,0:T(8,128)S(1)}, f32[3,8,24,128]{3,2,1,0:T(8,128)S(1)}, u32[]{:S(2)}, u32[]{:S(2)}) collective-permute-start(f32[3,8,24,128]{3,2,1,0:T(8,128)S(1)} %pad_maximum_fusion.67), channel_id=1, source_target_pairs={{0,496},{16,0},{32,16},{48,32},{64,48},{80,64},{96,80},{112,96},{1... | collective-permute-start | bytes 884744 | tf_op jit(solution)/shard_map/ppermute | solution.py:17
  76.8 4.7 %collective-permute-done.229 = f32[3,8,24,128]{3,2,1,0:T(8,128)S(1)} collective-permute-done((f32[3,8,24,128]{3,2,1,0:T(8,128)S(1)}, f32[3,8,24,128]{3,2,1,0:T(8,128)S(1)}, u32[]{:S(2)}, u32[]{:S(2)}) %collective-permute-start.229) | collective-permute-done | bytes 294944 | tf_op jit(solution)/shard_map/ppermute | solution.py:17
  81.5 1.1 fusion.47
  84.9 13.8 %conditional.6 = (f32[3,8,24,128]{3,2,1,0:T(8,128)}) conditional(s32[]{:T(128)} %clamp.15, (f32[3,8,24,256]{3,2,1,0:T(8,128)S(1)}) %tuple.490, (f32[3,8,24,256]{3,2,1,0:T(8,128)S(1)}) %tuple.490, (f32[3,8,24,256]{3,2,1,0:T(8,128)S(1)}) %tuple.490, (f32[3,8,24,256]{3,2,1,0:T(8,128)S(1)}) %tuple.490, ...), branch_computations={%region_66.67_spmd, %region_67.68_spmd, %region_68.69_spmd, %regio... | conditional | bytes 1769520 | solution.py:33
  85.0 1.9 %collective-permute-start.82 = (f32[3,8,24,128]{3,2,1,0:T(8,128)S(1)}, f32[3,8,24,128]{3,2,1,0:T(8,128)}, u32[]{:S(2)}, u32[]{:S(2)}) collective-permute-start(f32[3,8,24,128]{3,2,1,0:T(8,128)S(1)} %slice.1260), channel_id=1, source_target_pairs={{0,288},{16,304},{32,320},{48,336},{64,352},{80,368},{96,384},{112... | collective-permute-start | bytes 884744 | tf_op jit(solution)/shard_map/cond/branch_18_fun/ppermute | solution.py:17
  86.9 11.7 %collective-permute-done.82 = f32[3,8,24,128]{3,2,1,0:T(8,128)} collective-permute-done((f32[3,8,24,128]{3,2,1,0:T(8,128)S(1)}, f32[3,8,24,128]{3,2,1,0:T(8,128)}, u32[]{:S(2)}, u32[]{:S(2)}) %collective-permute-start.82) | collective-permute-done | bytes 294944 | tf_op jit(solution)/shard_map/cond/branch_18_fun/ppermute | solution.py:17
  99.7 1.9 %collective-permute-start.230 = (f32[3,6,24,128]{3,2,1,0:T(8,128)S(1)}, f32[3,6,24,128]{3,2,1,0:T(8,128)S(1)}, u32[]{:S(2)}, u32[]{:S(2)}) collective-permute-start(f32[3,6,24,128]{3,2,1,0:T(8,128)S(1)} %pad_maximum_fusion.68), channel_id=1, source_target_pairs={{0,16},{16,32},{32,48},{48,64},{64,80},{80,96},{96,112},{112,128},... | collective-permute-start | bytes 663560 | tf_op jit(solution)/shard_map/ppermute | solution.py:17
  101.7 3.3 %collective-permute-start.231 = (f32[3,6,24,128]{3,2,1,0:T(8,128)S(1)}, f32[3,6,24,128]{3,2,1,0:T(8,128)S(1)}, u32[]{:S(2)}, u32[]{:S(2)}) collective-permute-start(f32[3,6,24,128]{3,2,1,0:T(8,128)S(1)} %pad_maximum_fusion.69), channel_id=1, source_target_pairs={{0,496},{16,0},{32,16},{48,32},{64,48},{80,64},{96,80},{112,96},{1... | collective-permute-start | bytes 663560 | tf_op jit(solution)/shard_map/ppermute | solution.py:17
  105.6 1.4 %fusion.33 = (f32[3,8,24,256]{3,2,1,0:T(8,128)S(1)}, f32[3,8,24,256]{3,2,1,0:T(8,128)}, f32[3,8,24,256]{3,2,1,0:T(8,128)}) fusion(f32[3,8,24,256]{3,2,1,0:T(8,128)S(1)} %slice.1312, f32[3,12,24,256]{3,2,1,0:T(8,128)S(1)} %convolution_add_fusion), kind=kLoop, calls=%fused_computation.140 | loop fusion | flops 442368 | bytes 3538944 | tf_op jit(solution)/shard_map/add | solution.py:94
  107.0 2.2 %collective-permute-done.231 = f32[3,6,24,128]{3,2,1,0:T(8,128)S(1)} collective-permute-done((f32[3,6,24,128]{3,2,1,0:T(8,128)S(1)}, f32[3,6,24,128]{3,2,1,0:T(8,128)S(1)}, u32[]{:S(2)}, u32[]{:S(2)}) %collective-permute-start.231) | collective-permute-done | bytes 221216 | tf_op jit(solution)/shard_map/ppermute | solution.py:17
  112.2 15.8 %conditional.7 = (f32[3,11,16,128]{3,2,1,0:T(8,128)S(1)}) conditional(s32[]{:T(128)} %clamp.14, f32[3,8,16,128]{3,2,1,0:T(8,128)S(1)} %get-tuple-element.417, f32[3,8,16,128]{3,2,1,0:T(8,128)S(1)} %get-tuple-element.417, f32[3,8,16,128]{3,2,1,0:T(8,128)S(1)} %get-tuple-element.417, ...), branch_computations={%region_98.99_spmd, %region_99.100_spmd, %region_100.101_spmd, %re... | conditional | flops 67584 | bytes 2162776 | solution.py:52
  112.3 2.1 %collective-permute-start.106 = (f32[3,7,16,128]{3,2,1,0:T(8,128)S(1)}, f32[3,7,16,128]{3,2,1,0:T(8,128)S(1)}, u32[]{:S(2)}, u32[]{:S(2)}) collective-permute-start(f32[3,7,16,128]{3,2,1,0:T(8,128)S(1)} %slice.911), channel_id=1, source_target_pairs={{0,48},{16,64},{32,80},{48,96},{64,112},{80,128},{96,144},{112,160... | collective-permute-start | bytes 516104 | tf_op jit(solution)/shard_map/cond/branch_5_fun/ppermute | solution.py:17
  114.4 1.9 %collective-permute-start.107 = (f32[3,4,16,128]{3,2,1,0:T(8,128)S(1)}, f32[3,4,16,128]{3,2,1,0:T(8,128)S(1)}, u32[]{:S(2)}, u32[]{:S(2)}) collective-permute-start(f32[3,4,16,128]{3,2,1,0:T(8,128)S(1)} %slice.912), channel_id=1, source_target_pairs={{0,32},{16,48},{32,64},{48,80},{64,96},{80,112},{96,128},{112,144}... | collective-permute-start | bytes 294920 | tf_op jit(solution)/shard_map/cond/branch_5_fun/ppermute | solution.py:17
  116.3 11.4 %collective-permute-done.107 = f32[3,4,16,128]{3,2,1,0:T(8,128)S(1)} collective-permute-done((f32[3,4,16,128]{3,2,1,0:T(8,128)S(1)}, f32[3,4,16,128]{3,2,1,0:T(8,128)S(1)}, u32[]{:S(2)}, u32[]{:S(2)}) %collective-permute-start.107) | collective-permute-done | bytes 98336 | tf_op jit(solution)/shard_map/cond/branch_5_fun/ppermute | solution.py:17
  128.1 1.1 fusion.57
  (123 shorter events, 16.9 us)
Async XLA Ops:
  3.8 18.7 %collective-permute-start.29 = (f32[3,8,16,128]{3,2,1,0:T(8,128)S(1)}, f32[3,8,16,128]{3,2,1,0:T(8,128)S(1)}, u32[]{:S(2)}, u32[]{:S(2)}) collective-permute-start(f32[3,8,16,128]{3,2,1,0:T(8,128)S(1)} %param.29), channel_id=1, source_target_pairs={{0,464},{16,480},{32,496},{48,0},{64,16},{80,32},{96,48},{112,64},... | collective-permute-start | bytes 589832 | tf_op jit(solution)/shard_map/cond/branch_29_fun/ppermute | solution.py:17
  22.5 0.9 copy-start.4
  22.5 1.1 copy-start.3
  23.8 9.8 %copy-start.11 = (bf16[256,8]{0,1:T(8,128)(2,1)S(1)}, bf16[256,8]{0,1:T(8,128)(2,1)}, u32[]{:S(2)}) copy-start(bf16[256,8]{0,1:T(8,128)(2,1)} %param.169) | copy-start | bytes 12292
  23.8 10.6 %collective-permute-start.224 = (f32[3,8,8,256]{3,1,0,2:T(8,128)S(1)}, f32[3,8,8,256]{3,1,0,2:T(8,128)S(1)}, u32[]{:S(2)}, u32[]{:S(2)}) collective-permute-start(f32[3,8,8,256]{3,1,0,2:T(8,128)S(1)} %maximum_maximum_fusion.3), channel_id=1, source_target_pairs={{0,1},{1,2},{2,3},{3,4},{4,5},{5,6},{6,7},{7,8},{8,9},{9,10},{10,1... | collective-permute-start | bytes 589832 | tf_op jit(solution)/shard_map/ppermute | solution.py:22
  28.6 11.3 %collective-permute-start.225 = (f32[3,8,8,256]{3,2,1,0:T(8,128)S(1)}, f32[3,8,8,256]{3,2,1,0:T(8,128)S(1)}, u32[]{:S(2)}, u32[]{:S(2)}) collective-permute-start(f32[3,8,8,256]{3,2,1,0:T(8,128)S(1)} %maximum_maximum_fusion.4), channel_id=1, source_target_pairs={{1,0},{2,1},{3,2},{4,3},{5,4},{6,5},{7,6},{8,7},{9,8},{10,9},{11,1... | collective-permute-start | bytes 589832 | tf_op jit(solution)/shard_map/ppermute | solution.py:22
  39.9 0.7 copy-start.8
  41.4 7.3 %collective-permute-start.226 = (f32[3,10,24,128]{3,2,1,0:T(8,128)S(1)}, f32[3,10,24,128]{3,2,1,0:T(8,128)S(1)}, u32[]{:S(2)}, u32[]{:S(2)}) collective-permute-start(f32[3,10,24,128]{3,2,1,0:T(8,128)S(1)} %get-tuple-element.409), channel_id=1, source_target_pairs={{0,16},{16,32},{32,48},{48,64},{64,80},{80,96},{96,112},{112,128},... | collective-permute-start | bytes 1105928 | tf_op jit(solution)/shard_map/ppermute | solution.py:17
  43.3 9.1 %collective-permute-start.227 = (f32[3,10,24,128]{3,2,1,0:T(8,128)S(1)}, f32[3,10,24,128]{3,2,1,0:T(8,128)S(1)}, u32[]{:S(2)}, u32[]{:S(2)}) collective-permute-start(f32[3,10,24,128]{3,2,1,0:T(8,128)S(1)} %get-tuple-element.410), channel_id=1, source_target_pairs={{0,496},{16,0},{32,16},{48,32},{64,48},{80,64},{96,80},{112,96},{1... | collective-permute-start | bytes 1105928 | tf_op jit(solution)/shard_map/ppermute | solution.py:17
  48.8 3.8 %copy-start.7 = (f32[3,10,24,128]{3,2,1,0:T(8,128)}, f32[3,10,24,128]{3,2,1,0:T(8,128)S(1)}, u32[]{:S(2)}) copy-start(f32[3,10,24,128]{3,2,1,0:T(8,128)S(1)} %collective-permute-done.226) | copy-start | bytes 1105924
  48.8 3.8 %copy-start.9 = (bf16[256,8]{1,0:T(8,128)(2,1)S(1)}, bf16[256,8]{1,0:T(8,128)(2,1)}, u32[]{:S(2)}) copy-start(bf16[256,8]{1,0:T(8,128)(2,1)} %copy.16) | copy-start | bytes 12292
  53.0 0.9 copy-start
  54.4 1.1 slice-start
  57.4 12.7 %collective-permute-start.46 = (f32[3,8,24,128]{3,2,1,0:T(8,128)S(1)}, f32[3,8,24,128]{3,2,1,0:T(8,128)}, u32[]{:S(2)}, u32[]{:S(2)}) collective-permute-start(f32[3,8,24,128]{3,2,1,0:T(8,128)S(1)} %slice.1224), channel_id=1, source_target_pairs={{0,224},{16,240},{32,256},{48,272},{64,288},{80,304},{96,320},{112... | collective-permute-start | bytes 884744 | tf_op jit(solution)/shard_map/cond/branch_14_fun/ppermute | solution.py:17
  71.2 5.6 %collective-permute-start.228 = (f32[3,8,24,128]{3,2,1,0:T(8,128)S(1)}, f32[3,8,24,128]{3,2,1,0:T(8,128)S(1)}, u32[]{:S(2)}, u32[]{:S(2)}) collective-permute-start(f32[3,8,24,128]{3,2,1,0:T(8,128)S(1)} %pad_maximum_fusion.66), channel_id=1, source_target_pairs={{0,16},{16,32},{32,48},{48,64},{64,80},{80,96},{96,112},{112,128},... | collective-permute-start | bytes 884744 | tf_op jit(solution)/shard_map/ppermute | solution.py:17
  73.2 8.3 %collective-permute-start.229 = (f32[3,8,24,128]{3,2,1,0:T(8,128)S(1)}, f32[3,8,24,128]{3,2,1,0:T(8,128)S(1)}, u32[]{:S(2)}, u32[]{:S(2)}) collective-permute-start(f32[3,8,24,128]{3,2,1,0:T(8,128)S(1)} %pad_maximum_fusion.67), channel_id=1, source_target_pairs={{0,496},{16,0},{32,16},{48,32},{64,48},{80,64},{96,80},{112,96},{1... | collective-permute-start | bytes 884744 | tf_op jit(solution)/shard_map/ppermute | solution.py:17
  76.8 5.8 %copy-start.10 = (bf16[256,8]{1,0:T(8,128)(2,1)S(1)}, bf16[256,8]{1,0:T(8,128)(2,1)}, u32[]{:S(2)}) copy-start(bf16[256,8]{1,0:T(8,128)(2,1)} %copy.16) | copy-start | bytes 12292
  85.0 13.7 %collective-permute-start.82 = (f32[3,8,24,128]{3,2,1,0:T(8,128)S(1)}, f32[3,8,24,128]{3,2,1,0:T(8,128)}, u32[]{:S(2)}, u32[]{:S(2)}) collective-permute-start(f32[3,8,24,128]{3,2,1,0:T(8,128)S(1)} %slice.1260), channel_id=1, source_target_pairs={{0,288},{16,304},{32,320},{48,336},{64,352},{80,368},{96,384},{112... | collective-permute-start | bytes 884744 | tf_op jit(solution)/shard_map/cond/branch_18_fun/ppermute | solution.py:17
  99.7 7.3 %collective-permute-start.230 = (f32[3,6,24,128]{3,2,1,0:T(8,128)S(1)}, f32[3,6,24,128]{3,2,1,0:T(8,128)S(1)}, u32[]{:S(2)}, u32[]{:S(2)}) collective-permute-start(f32[3,6,24,128]{3,2,1,0:T(8,128)S(1)} %pad_maximum_fusion.68), channel_id=1, source_target_pairs={{0,16},{16,32},{32,48},{48,64},{64,80},{80,96},{96,112},{112,128},... | collective-permute-start | bytes 663560 | tf_op jit(solution)/shard_map/ppermute | solution.py:17
  101.7 7.5 %collective-permute-start.231 = (f32[3,6,24,128]{3,2,1,0:T(8,128)S(1)}, f32[3,6,24,128]{3,2,1,0:T(8,128)S(1)}, u32[]{:S(2)}, u32[]{:S(2)}) collective-permute-start(f32[3,6,24,128]{3,2,1,0:T(8,128)S(1)} %pad_maximum_fusion.69), channel_id=1, source_target_pairs={{0,496},{16,0},{32,16},{48,32},{64,48},{80,64},{96,80},{112,96},{1... | collective-permute-start | bytes 663560 | tf_op jit(solution)/shard_map/ppermute | solution.py:17
  110.6 0.9 copy-start.6
  112.2 15.8 %copy-start.1 = (f32[3,8,24,256]{3,2,1,0:T(8,128)S(1)}, f32[3,8,24,256]{3,2,1,0:T(8,128)}, u32[]{:S(2)}) copy-start(f32[3,8,24,256]{3,2,1,0:T(8,128)} %get-tuple-element.403) | copy-start | bytes 1769476
  112.2 15.8 %copy-start.2 = (f32[3,8,24,256]{3,2,1,0:T(8,128)S(1)}, f32[3,8,24,256]{3,2,1,0:T(8,128)}, u32[]{:S(2)}) copy-start(f32[3,8,24,256]{3,2,1,0:T(8,128)} %get-tuple-element.404) | copy-start | bytes 1769476
  112.2 15.8 %copy-start.5 = (f32[8,16,256]{2,1,0:T(8,128)S(1)}, f32[8,16,256]{2,1,0:T(8,128)}, u32[]{:S(2)}) copy-start(f32[8,16,256]{2,1,0:T(8,128)} %slice.1323) | copy-start | bytes 393220
  112.3 15.4 %collective-permute-start.106 = (f32[3,7,16,128]{3,2,1,0:T(8,128)S(1)}, f32[3,7,16,128]{3,2,1,0:T(8,128)S(1)}, u32[]{:S(2)}, u32[]{:S(2)}) collective-permute-start(f32[3,7,16,128]{3,2,1,0:T(8,128)S(1)} %slice.911), channel_id=1, source_target_pairs={{0,48},{16,64},{32,80},{48,96},{64,112},{80,128},{96,144},{112,160... | collective-permute-start | bytes 516104 | tf_op jit(solution)/shard_map/cond/branch_5_fun/ppermute | solution.py:17
  114.4 13.3 %collective-permute-start.107 = (f32[3,4,16,128]{3,2,1,0:T(8,128)S(1)}, f32[3,4,16,128]{3,2,1,0:T(8,128)S(1)}, u32[]{:S(2)}, u32[]{:S(2)}) collective-permute-start(f32[3,4,16,128]{3,2,1,0:T(8,128)S(1)} %slice.912), channel_id=1, source_target_pairs={{0,32},{16,48},{32,64},{48,80},{64,96},{80,112},{96,128},{112,144}... | collective-permute-start | bytes 294920 | tf_op jit(solution)/shard_map/cond/branch_5_fun/ppermute | solution.py:17
where the time goes:
time: 130 us; the launch traced here: 129 us
  waiting for transfers between devices  50.6 us (39%)
  starting transfers between devices  47.9 us (37%)
  local copies, waits for them, and re-layouts  14.4 us (11%)
  other arithmetic  9.69 us (7%)
  between operations  4.82 us (4%)
    ppermute x11, waiting for transfers between devices, shifted(): return lax.ppermute(x, axis, [(i, (i + by) % peers) for i in range(peers)])  45.1 us
    ppermute x11, starting transfers between devices, shifted(): return lax.ppermute(x, axis, [(i, (i + by) % peers) for i in range(peers)])  41.1 us
    ppermute x2, starting transfers between devices, stepped(): lax.ppermute(x, axis, [(i, i + by) for i in range(peers) if 0 <= i + by <...  6.79 us
    ppermute x2, waiting for transfers between devices, stepped(): lax.ppermute(x, axis, [(i, i + by) for i in range(peers) if 0 <= i + by <...  5.46 us
    unnamed x30, local copies, waits for them, and re-layouts  3.44 us
  transfers between devices with their start and end apart: 13, of which 9 were waited for; matrix products, arithmetic and copies ran while one was open for 5% of the time, Pallas kernels for 0%

commit v1 on v0

--- a/solution.py
+++ b/solution.py
@@ -17,9 +17,23 @@
     return lax.ppermute(x, axis, [(i, (i + by) % peers) for i in range(peers)])
 
 
-def stepped(x, axis, by):
+def swapped(up, down, axis, wraps):
     peers = lax.axis_size(axis)
-    return lax.ppermute(x, axis, [(i, i + by) for i in range(peers) if 0 <= i + by < peers])
+    even = lax.axis_index(axis) % 2 == 0
+    within = [(i, i ^ 1) for i in range(peers)]
+    across = [(i, i + 1 if i % 2 else i - 1) for i in range(peers)]
+    if wraps:
+        across = [(i, j % peers) for i, j in across]
+    else:
+        across = [(i, j) for i, j in across if 0 <= j < peers]
+    inner, outer = jnp.where(even, up, down), jnp.where(even, down, up)
+    if wraps:
+        inner = lax.ppermute(inner, axis, within)
+        outer = lax.ppermute(outer, axis, across)
+    else:
+        outer = lax.ppermute(outer, axis, across)
+        inner = lax.ppermute(inner, axis, within)
+    return jnp.where(even, outer, inner), jnp.where(even, inner, outer)
 
 
 def nearest(shift, width):
@@ -61,8 +75,7 @@
     if extra is not None:
         up += [extra[:, -1:, :, :RB], extra[:, -1:, :, RB:]]
         down += [extra[:, :1, :, :RB], extra[:, :1, :, RB:]]
-    low = shifted(jnp.concatenate(up, axis=1), "theta", 1)
-    high = shifted(jnp.concatenate(down, axis=1), "theta", -1)
+    low, high = swapped(jnp.concatenate(up, axis=1), jnp.concatenate(down, axis=1), "theta", True)
     rotors = jnp.concatenate([low[:, :reach], rotor, high[:, :reach]], axis=1)
     aligned = lax.dynamic_slice_in_dim(rotors, reach - h - remain, width + 2 * h, axis=1)
     stators = jnp.concatenate([low[:, reach : reach + h], stator, high[:, reach : reach + h]], axis=1)
@@ -113,8 +126,9 @@
             [cut(field, ZH, 2), cut(seed, 2, 2), layers, jnp.zeros_like(layers)], axis=2
         )
 
-    low = stepped(packed(lambda x, n, d: lax.slice_in_dim(x, nz - n, nz, axis=d)), "gz", 1)
-    high = stepped(packed(lambda x, n, d: lax.slice_in_dim(x, 0, n, axis=d)), "gz", -1)
+    top = packed(lambda x, n, d: lax.slice_in_dim(x, nz - n, nz, axis=d))
+    bottom = packed(lambda x, n, d: lax.slice_in_dim(x, 0, n, axis=d))
+    low, high = swapped(top, bottom, "gz", False)
 
     def layers_of(x):
         return jnp.moveaxis(x[:, :, ZH + 2], 0, 1)

time: 130 us -> 126 us (0.969)
  the two profiles are of different devices: /device:TPU:29 before, /device:TPU:32 now
where the time goes in v1:
time: 126 us
  starting transfers between devices  48.7 us (39%)
  waiting for transfers between devices  45.3 us (36%)
  other arithmetic  14.3 us (11%)
  local copies, waits for them, and re-layouts  10.9 us (9%)
  between operations  4.74 us (4%)
    ppermute x5, waiting for transfers between devices, shifted(): return lax.ppermute(x, axis, [(i, (i + by) % peers) for i in range(peers)])  31.4 us
    ppermute x5, starting transfers between devices, shifted(): return lax.ppermute(x, axis, [(i, (i + by) % peers) for i in range(peers)])  19 us
    ppermute x4, starting transfers between devices, swapped(): outer = lax.ppermute(outer, axis, across)  17.4 us
    ppermute x4, starting transfers between devices, swapped(): inner = lax.ppermute(inner, axis, within)  12.3 us
    ppermute x4, waiting for transfers between devices, swapped(): outer = lax.ppermute(outer, axis, across)  9.32 us
    ppermute x4, waiting for transfers between devices, swapped(): inner = lax.ppermute(inner, axis, within)  4.55 us
  transfers between devices with their start and end apart: 13, of which 9 were waited for; matrix products, arithmetic and copies ran while one was open for 2% of the time, Pallas kernels for 0%

profile of v1, /device:TPU:32, one launch (start us, length us, event | category | flops | bytes accessed | tf_op | source)
XLA Modules:
  0.0 125.6 jit_solution(1754004137501518996)
XLA Ops:
  0.6 1.4 %fusion.100 = (s32[1]{0:T(128)}, s32[1]{0:T(128)}) fusion(s32[2]{0:T(128)} %param.167), kind=kLoop, calls=%fused_computation.264 | loop fusion | bytes 16 | tf_op jit(solution)/shard_map/slice | solution.py:150
  4.9 16.1 %conditional.4 = (f32[3,8,16,128]{3,2,1,0:T(8,128)}) conditional(s32[]{:T(128)} %clamp.13, f32[3,8,16,128]{3,2,1,0:T(8,128)S(1)} %get-tuple-element.432, f32[3,8,16,128]{3,2,1,0:T(8,128)S(1)} %get-tuple-element.432, f32[3,8,16,128]{3,2,1,0:T(8,128)S(1)} %get-tuple-element.432, ...), branch_computations={%region_0.1_spmd, %region_1.2_spmd, %region_2.3_spmd, %region_3.4_... | conditional | bytes 786480 | solution.py:47
  4.9 7.0 %collective-permute-start.20 = (f32[3,8,16,128]{3,2,1,0:T(8,128)S(1)}, f32[3,8,16,128]{3,2,1,0:T(8,128)}, u32[]{:S(2)}, u32[]{:S(2)}) collective-permute-start(f32[3,8,16,128]{3,2,1,0:T(8,128)S(1)} %param.20), channel_id=1, source_target_pairs={{0,320},{16,336},{32,352},{48,368},{64,384},{80,400},{96,416},{112... | collective-permute-start | bytes 589832 | tf_op jit(solution)/shard_map/cond/branch_20_fun/ppermute | solution.py:17
  11.9 9.1 %collective-permute-done.20 = f32[3,8,16,128]{3,2,1,0:T(8,128)} collective-permute-done((f32[3,8,16,128]{3,2,1,0:T(8,128)S(1)}, f32[3,8,16,128]{3,2,1,0:T(8,128)}, u32[]{:S(2)}, u32[]{:S(2)}) %collective-permute-start.20) | collective-permute-done | bytes 196640 | tf_op jit(solution)/shard_map/cond/branch_20_fun/ppermute | solution.py:17
  21.0 1.1 broadcast_select_fusion.10
  22.1 5.1 %collective-permute-start.225 = (f32[3,8,8,256]{3,2,1,0:T(8,128)S(1)}, f32[3,8,8,256]{3,2,1,0:T(8,128)S(1)}, u32[]{:S(2)}, u32[]{:S(2)}) collective-permute-start(f32[3,8,8,256]{3,2,1,0:T(8,128)S(1)} %get-tuple-element.420), channel_id=1, source_target_pairs={{0,1},{1,0},{2,3},{3,2},{4,5},{5,4},{6,7},{7,6},{8,9},{9,8},{10,11... | collective-permute-start | bytes 589832 | tf_op jit(solution)/shard_map/ppermute | solution.py:35
  27.2 2.3 %collective-permute-start.224 = (f32[3,8,8,256]{3,2,1,0:T(8,128)S(1)}, f32[3,8,8,256]{3,2,1,0:T(8,128)S(1)}, u32[]{:S(2)}, u32[]{:S(2)}) collective-permute-start(f32[3,8,8,256]{3,2,1,0:T(8,128)S(1)} %get-tuple-element.421), channel_id=1, source_target_pairs={{1,2},{2,1},{3,4},{4,3},{5,6},{6,5},{7,8},{8,7},{9,10},{10,9},{11,... | collective-permute-start | bytes 589832 | tf_op jit(solution)/shard_map/ppermute | solution.py:34
  30.4 4.5 %collective-permute-done.225 = f32[3,8,8,256]{3,2,1,0:T(8,128)S(1)} collective-permute-done((f32[3,8,8,256]{3,2,1,0:T(8,128)S(1)}, f32[3,8,8,256]{3,2,1,0:T(8,128)S(1)}, u32[]{:S(2)}, u32[]{:S(2)}) %collective-permute-start.225) | collective-permute-done | bytes 196640 | tf_op jit(solution)/shard_map/ppermute | solution.py:35
  35.0 3.5 %collective-permute-done.224 = f32[3,8,8,256]{3,2,1,0:T(8,128)S(1)} collective-permute-done((f32[3,8,8,256]{3,2,1,0:T(8,128)S(1)}, f32[3,8,8,256]{3,2,1,0:T(8,128)S(1)}, u32[]{:S(2)}, u32[]{:S(2)}) %collective-permute-start.224) | collective-permute-done | bytes 196640 | tf_op jit(solution)/shard_map/ppermute | solution.py:34
  41.6 7.2 %collective-permute-start.226 = (f32[3,10,24,128]{3,2,1,0:T(8,128)S(1)}, f32[3,10,24,128]{3,2,1,0:T(8,128)S(1)}, u32[]{:S(2)}, u32[]{:S(2)}) collective-permute-start(f32[3,10,24,128]{3,2,1,0:T(8,128)S(1)} %broadcast_select_fusion.3), channel_id=1, source_target_pairs={{0,496},{16,32},{32,16},{48,64},{64,48},{80,96},{96,80},{112,128},... | collective-permute-start | bytes 1105928 | tf_op jit(solution)/shard_map/ppermute | solution.py:32
  48.8 3.0 %collective-permute-start.227 = (f32[3,10,24,128]{3,2,1,0:T(8,128)S(1)}, f32[3,10,24,128]{3,2,1,0:T(8,128)S(1)}, u32[]{:S(2)}, u32[]{:S(2)}) collective-permute-start(f32[3,10,24,128]{3,2,1,0:T(8,128)S(1)} %broadcast_select_fusion.2), channel_id=1, source_target_pairs={{0,16},{16,0},{32,48},{48,32},{64,80},{80,64},{96,112},{112,96},{1... | collective-permute-start | bytes 1105928 | tf_op jit(solution)/shard_map/ppermute | solution.py:31
  52.0 2.0 %collective-permute-done.226 = f32[3,10,24,128]{3,2,1,0:T(8,128)S(1)} collective-permute-done((f32[3,10,24,128]{3,2,1,0:T(8,128)S(1)}, f32[3,10,24,128]{3,2,1,0:T(8,128)S(1)}, u32[]{:S(2)}, u32[]{:S(2)}) %collective-permute-start.226) | collective-permute-done | bytes 368672 | tf_op jit(solution)/shard_map/ppermute | solution.py:32
  57.1 1.8 %fusion.31 = f32[3,8,24,256]{3,2,1,0:T(8,128)S(1)} fusion(f32[3,8,24,256]{3,2,1,0:T(8,128)S(1)} %slice-done, f32[3,12,24,256]{3,2,1,0:T(8,128)} %copy-done, f32[8,24,256]{2,1,0:T(8,128)S(1)} %copy.10, f32[8,24,256]{2,1,0:T(8,128)S(1)} %slice_multiply_fusion.2, f32[24]{0:T(128)S(1)} %and_convert_fusion), kind=kLoop, calls=%fused_computation.138 | loop fusion | flops 1769472 | bytes 2752608 | tf_op jit(solution)/shard_map/mul | solution.py:163
  58.9 10.1 %conditional.5 = (f32[3,8,24,128]{3,2,1,0:T(8,128)}) conditional(s32[]{:T(128)} %clamp.12, (f32[3,8,24,256]{3,2,1,0:T(8,128)S(1)}) %tuple.489, (f32[3,8,24,256]{3,2,1,0:T(8,128)S(1)}) %tuple.489, (f32[3,8,24,256]{3,2,1,0:T(8,128)S(1)}) %tuple.489, (f32[3,8,24,256]{3,2,1,0:T(8,128)S(1)}) %tuple.489, ...), branch_computations={%region_33.34_spmd, %region_34.35_spmd, %region_35.36_spmd, %regio... | conditional | bytes 1769520 | solution.py:47
  59.0 5.7 %collective-permute-start.63 = (f32[3,8,24,128]{3,2,1,0:T(8,128)S(1)}, f32[3,8,24,128]{3,2,1,0:T(8,128)}, u32[]{:S(2)}, u32[]{:S(2)}) collective-permute-start(f32[3,8,24,128]{3,2,1,0:T(8,128)S(1)} %slice.1241), channel_id=1, source_target_pairs={{0,496},{16,0},{32,16},{48,32},{64,48},{80,64},{96,80},{112,96},{1... | collective-permute-start | bytes 884744 | tf_op jit(solution)/shard_map/cond/branch_31_fun/ppermute | solution.py:17
  64.8 4.2 %collective-permute-done.63 = f32[3,8,24,128]{3,2,1,0:T(8,128)} collective-permute-done((f32[3,8,24,128]{3,2,1,0:T(8,128)S(1)}, f32[3,8,24,128]{3,2,1,0:T(8,128)}, u32[]{:S(2)}, u32[]{:S(2)}) %collective-permute-start.63) | collective-permute-done | bytes 294944 | tf_op jit(solution)/shard_map/cond/branch_31_fun/ppermute | solution.py:17
  69.0 1.1 fusion.99
  70.9 6.0 %collective-permute-start.228 = (f32[3,8,24,128]{3,2,1,0:T(8,128)}, f32[3,8,24,128]{3,2,1,0:T(8,128)S(1)}, u32[]{:S(2)}, u32[]{:S(2)}) collective-permute-start(f32[3,8,24,128]{3,2,1,0:T(8,128)} %get-tuple-element.408), channel_id=1, source_target_pairs={{0,496},{16,32},{32,16},{48,64},{64,48},{80,96},{96,80},{112,128},... | collective-permute-start | bytes 884744 | tf_op jit(solution)/shard_map/ppermute | solution.py:32
  77.0 2.1 %collective-permute-start.229 = (f32[3,8,24,128]{3,2,1,0:T(8,128)}, f32[3,8,24,128]{3,2,1,0:T(8,128)}, u32[]{:S(2)}, u32[]{:S(2)}) collective-permute-start(f32[3,8,24,128]{3,2,1,0:T(8,128)} %get-tuple-element.409), channel_id=1, source_target_pairs={{0,16},{16,0},{32,48},{48,32},{64,80},{80,64},{96,112},{112,96},{1... | collective-permute-start | bytes 884744 | tf_op jit(solution)/shard_map/ppermute | solution.py:31
  82.9 1.1 fusion.47
  86.9 10.3 %conditional.6 = (f32[3,8,24,128]{3,2,1,0:T(8,128)}) conditional(s32[]{:T(128)} %clamp.15, (f32[3,8,24,256]{3,2,1,0:T(8,128)S(1)}) %tuple.490, (f32[3,8,24,256]{3,2,1,0:T(8,128)S(1)}) %tuple.490, (f32[3,8,24,256]{3,2,1,0:T(8,128)S(1)}) %tuple.490, (f32[3,8,24,256]{3,2,1,0:T(8,128)S(1)}) %tuple.490, ...), branch_computations={%region_66.67_spmd, %region_67.68_spmd, %region_68.69_spmd, %regio... | conditional | bytes 1769520 | solution.py:47
  87.0 2.4 %collective-permute-start.65 = (f32[3,8,24,128]{3,2,1,0:T(8,128)S(1)}, f32[3,8,24,128]{3,2,1,0:T(8,128)}, u32[]{:S(2)}, u32[]{:S(2)}) collective-permute-start(f32[3,8,24,128]{3,2,1,0:T(8,128)S(1)} %slice.1243), channel_id=1, source_target_pairs={{0,16},{16,32},{32,48},{48,64},{64,80},{80,96},{96,112},{112,128},... | collective-permute-start | bytes 884744 | tf_op jit(solution)/shard_map/cond/branch_1_fun/ppermute | solution.py:17
  89.4 7.8 %collective-permute-done.65 = f32[3,8,24,128]{3,2,1,0:T(8,128)} collective-permute-done((f32[3,8,24,128]{3,2,1,0:T(8,128)S(1)}, f32[3,8,24,128]{3,2,1,0:T(8,128)}, u32[]{:S(2)}, u32[]{:S(2)}) %collective-permute-start.65) | collective-permute-done | bytes 294944 | tf_op jit(solution)/shard_map/cond/branch_1_fun/ppermute | solution.py:17
  98.3 1.9 %collective-permute-start.230 = (f32[3,6,24,128]{3,2,1,0:T(8,128)S(1)}, f32[3,6,24,128]{3,2,1,0:T(8,128)S(1)}, u32[]{:S(2)}, u32[]{:S(2)}) collective-permute-start(f32[3,6,24,128]{3,2,1,0:T(8,128)S(1)} %get-tuple-element.424), channel_id=1, source_target_pairs={{0,496},{16,32},{32,16},{48,64},{64,48},{80,96},{96,80},{112,128},... | collective-permute-start | bytes 663560 | tf_op jit(solution)/shard_map/ppermute | solution.py:32
  100.2 2.1 %collective-permute-start.231 = (f32[3,6,24,128]{3,2,1,0:T(8,128)S(1)}, f32[3,6,24,128]{3,2,1,0:T(8,128)S(1)}, u32[]{:S(2)}, u32[]{:S(2)}) collective-permute-start(f32[3,6,24,128]{3,2,1,0:T(8,128)S(1)} %get-tuple-element.425), channel_id=1, source_target_pairs={{0,16},{16,0},{32,48},{48,32},{64,80},{80,64},{96,112},{112,96},{1... | collective-permute-start | bytes 663560 | tf_op jit(solution)/shard_map/ppermute | solution.py:31
  102.8 1.1 fusion.57
  103.8 3.8 %collective-permute-done.230 = f32[3,6,24,128]{3,2,1,0:T(8,128)S(1)} collective-permute-done((f32[3,6,24,128]{3,2,1,0:T(8,128)S(1)}, f32[3,6,24,128]{3,2,1,0:T(8,128)S(1)}, u32[]{:S(2)}, u32[]{:S(2)}) %collective-permute-start.230) | collective-permute-done | bytes 221216 | tf_op jit(solution)/shard_map/ppermute | solution.py:32
  110.2 14.5 %conditional.7 = (f32[3,11,16,128]{3,2,1,0:T(8,128)S(1)}) conditional(s32[]{:T(128)} %clamp.14, f32[3,8,16,128]{3,2,1,0:T(8,128)S(1)} %get-tuple-element.426, f32[3,8,16,128]{3,2,1,0:T(8,128)S(1)} %get-tuple-element.426, f32[3,8,16,128]{3,2,1,0:T(8,128)S(1)} %get-tuple-element.426, ...), branch_computations={%region_98.99_spmd, %region_99.100_spmd, %region_100.101_spmd, %re... | conditional | flops 67584 | bytes 2162776 | solution.py:66
  110.3 1.9 %collective-permute-start.142 = (f32[3,7,16,128]{3,2,1,0:T(8,128)S(1)}, f32[3,7,16,128]{3,2,1,0:T(8,128)S(1)}, u32[]{:S(2)}, u32[]{:S(2)}) collective-permute-start(f32[3,7,16,128]{3,2,1,0:T(8,128)S(1)} %slice.938), channel_id=1, source_target_pairs={{0,192},{16,208},{32,224},{48,240},{64,256},{80,272},{96,288},{112... | collective-permute-start | bytes 516104 | tf_op jit(solution)/shard_map/cond/branch_23_fun/ppermute | solution.py:17
  112.3 1.9 %collective-permute-start.143 = (f32[3,4,16,128]{3,2,1,0:T(8,128)S(1)}, f32[3,4,16,128]{3,2,1,0:T(8,128)S(1)}, u32[]{:S(2)}, u32[]{:S(2)}) collective-permute-start(f32[3,4,16,128]{3,2,1,0:T(8,128)S(1)} %slice.939), channel_id=1, source_target_pairs={{0,176},{16,192},{32,208},{48,224},{64,240},{80,256},{96,272},{112... | collective-permute-start | bytes 294920 | tf_op jit(solution)/shard_map/cond/branch_23_fun/ppermute | solution.py:17
  114.2 8.9 %collective-permute-done.143 = f32[3,4,16,128]{3,2,1,0:T(8,128)S(1)} collective-permute-done((f32[3,4,16,128]{3,2,1,0:T(8,128)S(1)}, f32[3,4,16,128]{3,2,1,0:T(8,128)S(1)}, u32[]{:S(2)}, u32[]{:S(2)}) %collective-permute-start.143) | collective-permute-done | bytes 98336 | tf_op jit(solution)/shard_map/cond/branch_23_fun/ppermute | solution.py:17
  123.1 1.4 %collective-permute-done.142 = f32[3,7,16,128]{3,2,1,0:T(8,128)S(1)} collective-permute-done((f32[3,7,16,128]{3,2,1,0:T(8,128)S(1)}, f32[3,7,16,128]{3,2,1,0:T(8,128)S(1)}, u32[]{:S(2)}, u32[]{:S(2)}) %collective-permute-start.142) | collective-permute-done | bytes 172064 | tf_op jit(solution)/shard_map/cond/branch_23_fun/ppermute | solution.py:17
  (112 shorter events, 18.9 us)
Async XLA Ops:
  0.6 4.2 %copy-start.5 = (f32[3,8,16,256]{3,2,1,0:T(8,128)S(1)}, f32[3,8,16,256]{3,2,1,0:T(8,128)}, u32[]{:S(2)}) copy-start(f32[3,8,16,256]{3,2,1,0:T(8,128)} %param.165) | copy-start | bytes 1179652
  4.8 25.4 %copy-start.8 = (bf16[256,8]{0,1:T(8,128)(2,1)S(1)}, bf16[256,8]{0,1:T(8,128)(2,1)}, u32[]{:S(2)}) copy-start(bf16[256,8]{0,1:T(8,128)(2,1)} %param.169) | copy-start | bytes 12292
  4.9 16.1 %collective-permute-start.20 = (f32[3,8,16,128]{3,2,1,0:T(8,128)S(1)}, f32[3,8,16,128]{3,2,1,0:T(8,128)}, u32[]{:S(2)}, u32[]{:S(2)}) collective-permute-start(f32[3,8,16,128]{3,2,1,0:T(8,128)S(1)} %param.20), channel_id=1, source_target_pairs={{0,320},{16,336},{32,352},{48,368},{64,384},{80,400},{96,416},{112... | collective-permute-start | bytes 589832 | tf_op jit(solution)/shard_map/cond/branch_20_fun/ppermute | solution.py:17
  22.1 16.6 %copy-start.1 = (f32[3,8,16,256]{3,2,1,0:T(8,128)S(1)}, f32[3,8,16,256]{3,2,1,0:T(8,128)}, u32[]{:S(2)}) copy-start(f32[3,8,16,256]{3,2,1,0:T(8,128)} %param.166) | copy-start | bytes 1179652
  22.1 12.8 %collective-permute-start.225 = (f32[3,8,8,256]{3,2,1,0:T(8,128)S(1)}, f32[3,8,8,256]{3,2,1,0:T(8,128)S(1)}, u32[]{:S(2)}, u32[]{:S(2)}) collective-permute-start(f32[3,8,8,256]{3,2,1,0:T(8,128)S(1)} %get-tuple-element.420), channel_id=1, source_target_pairs={{0,1},{1,0},{2,3},{3,2},{4,5},{5,4},{6,7},{7,6},{8,9},{9,8},{10,11... | collective-permute-start | bytes 589832 | tf_op jit(solution)/shard_map/ppermute | solution.py:35
  27.2 11.3 %collective-permute-start.224 = (f32[3,8,8,256]{3,2,1,0:T(8,128)S(1)}, f32[3,8,8,256]{3,2,1,0:T(8,128)S(1)}, u32[]{:S(2)}, u32[]{:S(2)}) collective-permute-start(f32[3,8,8,256]{3,2,1,0:T(8,128)S(1)} %get-tuple-element.421), channel_id=1, source_target_pairs={{1,2},{2,1},{3,4},{4,3},{5,6},{6,5},{7,8},{8,7},{9,10},{10,9},{11,... | collective-permute-start | bytes 589832 | tf_op jit(solution)/shard_map/ppermute | solution.py:34
  30.4 23.9 %copy-start.6 = (bf16[256,8]{1,0:T(8,128)(2,1)}, bf16[256,8]{1,0:T(8,128)(2,1)S(1)}, u32[]{:S(2)}) copy-start(bf16[256,8]{1,0:T(8,128)(2,1)S(1)} %copy.9) | copy-start | bytes 12292
  40.6 0.9 copy-start.2
  41.6 12.4 %collective-permute-start.226 = (f32[3,10,24,128]{3,2,1,0:T(8,128)S(1)}, f32[3,10,24,128]{3,2,1,0:T(8,128)S(1)}, u32[]{:S(2)}, u32[]{:S(2)}) collective-permute-start(f32[3,10,24,128]{3,2,1,0:T(8,128)S(1)} %broadcast_select_fusion.3), channel_id=1, source_target_pairs={{0,496},{16,32},{32,16},{48,64},{64,48},{80,96},{96,80},{112,128},... | collective-permute-start | bytes 1105928 | tf_op jit(solution)/shard_map/ppermute | solution.py:32
  48.8 5.2 %collective-permute-start.227 = (f32[3,10,24,128]{3,2,1,0:T(8,128)S(1)}, f32[3,10,24,128]{3,2,1,0:T(8,128)S(1)}, u32[]{:S(2)}, u32[]{:S(2)}) collective-permute-start(f32[3,10,24,128]{3,2,1,0:T(8,128)S(1)} %broadcast_select_fusion.2), channel_id=1, source_target_pairs={{0,16},{16,0},{32,48},{48,32},{64,80},{80,64},{96,112},{112,96},{1... | collective-permute-start | bytes 1105928 | tf_op jit(solution)/shard_map/ppermute | solution.py:31
  54.6 0.9 copy-start
  56.1 1.1 slice-start
  59.0 10.0 %collective-permute-start.63 = (f32[3,8,24,128]{3,2,1,0:T(8,128)S(1)}, f32[3,8,24,128]{3,2,1,0:T(8,128)}, u32[]{:S(2)}, u32[]{:S(2)}) collective-permute-start(f32[3,8,24,128]{3,2,1,0:T(8,128)S(1)} %slice.1241), channel_id=1, source_target_pairs={{0,496},{16,0},{32,16},{48,32},{64,48},{80,64},{96,80},{112,96},{1... | collective-permute-start | bytes 884744 | tf_op jit(solution)/shard_map/cond/branch_31_fun/ppermute | solution.py:17
  70.9 10.8 %collective-permute-start.228 = (f32[3,8,24,128]{3,2,1,0:T(8,128)}, f32[3,8,24,128]{3,2,1,0:T(8,128)S(1)}, u32[]{:S(2)}, u32[]{:S(2)}) collective-permute-start(f32[3,8,24,128]{3,2,1,0:T(8,128)} %get-tuple-element.408), channel_id=1, source_target_pairs={{0,496},{16,32},{32,16},{48,64},{64,48},{80,96},{96,80},{112,128},... | collective-permute-start | bytes 884744 | tf_op jit(solution)/shard_map/ppermute | solution.py:32
  77.0 4.8 %collective-permute-start.229 = (f32[3,8,24,128]{3,2,1,0:T(8,128)}, f32[3,8,24,128]{3,2,1,0:T(8,128)}, u32[]{:S(2)}, u32[]{:S(2)}) collective-permute-start(f32[3,8,24,128]{3,2,1,0:T(8,128)} %get-tuple-element.409), channel_id=1, source_target_pairs={{0,16},{16,0},{32,48},{48,32},{64,80},{80,64},{96,112},{112,96},{1... | collective-permute-start | bytes 884744 | tf_op jit(solution)/shard_map/ppermute | solution.py:31
  82.9 1.1 copy-start.7
  87.0 10.3 %collective-permute-start.65 = (f32[3,8,24,128]{3,2,1,0:T(8,128)S(1)}, f32[3,8,24,128]{3,2,1,0:T(8,128)}, u32[]{:S(2)}, u32[]{:S(2)}) collective-permute-start(f32[3,8,24,128]{3,2,1,0:T(8,128)S(1)} %slice.1243), channel_id=1, source_target_pairs={{0,16},{16,32},{32,48},{48,64},{64,80},{80,96},{96,112},{112,128},... | collective-permute-start | bytes 884744 | tf_op jit(solution)/shard_map/cond/branch_1_fun/ppermute | solution.py:17
  98.3 9.4 %collective-permute-start.230 = (f32[3,6,24,128]{3,2,1,0:T(8,128)S(1)}, f32[3,6,24,128]{3,2,1,0:T(8,128)S(1)}, u32[]{:S(2)}, u32[]{:S(2)}) collective-permute-start(f32[3,6,24,128]{3,2,1,0:T(8,128)S(1)} %get-tuple-element.424), channel_id=1, source_target_pairs={{0,496},{16,32},{32,16},{48,64},{64,48},{80,96},{96,80},{112,128},... | collective-permute-start | bytes 663560 | tf_op jit(solution)/shard_map/ppermute | solution.py:32
  100.2 2.5 %copy-start.3 = (f32[8,16,256]{2,1,0:T(8,128)S(1)}, f32[8,16,256]{2,1,0:T(8,128)}, u32[]{:S(2)}) copy-start(f32[8,16,256]{2,1,0:T(8,128)} %slice.1322) | copy-start | bytes 393220
  100.2 2.5 %copy-start.4 = (f32[8,16,256]{2,1,0:T(8,128)S(1)}, f32[8,16,256]{2,1,0:T(8,128)}, u32[]{:S(2)}) copy-start(f32[8,16,256]{2,1,0:T(8,128)} %slice.1321) | copy-start | bytes 393220
  100.2 7.4 %collective-permute-start.231 = (f32[3,6,24,128]{3,2,1,0:T(8,128)S(1)}, f32[3,6,24,128]{3,2,1,0:T(8,128)S(1)}, u32[]{:S(2)}, u32[]{:S(2)}) collective-permute-start(f32[3,6,24,128]{3,2,1,0:T(8,128)S(1)} %get-tuple-element.425), channel_id=1, source_target_pairs={{0,16},{16,0},{32,48},{48,32},{64,80},{80,64},{96,112},{112,96},{1... | collective-permute-start | bytes 663560 | tf_op jit(solution)/shard_map/ppermute | solution.py:31
  110.3 14.2 %collective-permute-start.142 = (f32[3,7,16,128]{3,2,1,0:T(8,128)S(1)}, f32[3,7,16,128]{3,2,1,0:T(8,128)S(1)}, u32[]{:S(2)}, u32[]{:S(2)}) collective-permute-start(f32[3,7,16,128]{3,2,1,0:T(8,128)S(1)} %slice.938), channel_id=1, source_target_pairs={{0,192},{16,208},{32,224},{48,240},{64,256},{80,272},{96,288},{112... | collective-permute-start | bytes 516104 | tf_op jit(solution)/shard_map/cond/branch_23_fun/ppermute | solution.py:17
  112.3 10.8 %collective-permute-start.143 = (f32[3,4,16,128]{3,2,1,0:T(8,128)S(1)}, f32[3,4,16,128]{3,2,1,0:T(8,128)S(1)}, u32[]{:S(2)}, u32[]{:S(2)}) collective-permute-start(f32[3,4,16,128]{3,2,1,0:T(8,128)S(1)} %slice.939), channel_id=1, source_target_pairs={{0,176},{16,192},{32,208},{48,224},{64,240},{80,256},{96,272},{112... | collective-permute-start | bytes 294920 | tf_op jit(solution)/shard_map/cond/branch_23_fun/ppermute | solution.py:17

commit v2 on v0

v2 whole, which is shorter than its diff:
```python
import jax
import jax.numpy as jnp
from jax import lax
from jax.experimental import pallas as pl
from jax.experimental.pallas import tpu as pltpu
from jax.sharding import PartitionSpec as P

NR = 256
RB = 128
BAND = 8
STEPS = 2
LOWER = RB - BAND // 2
UPPER = RB + BAND // 2
ZH = 4


def is_even(axis):
    return 1 - lax.rem(lax.axis_index(axis), 2)


def left_over(shift, width):
    half = width // 2
    return ((shift + half) & (width - 1)) - half


def call(kernel, outs, offsets, *arrays, scratch=()):
    whole = pl.BlockSpec(memory_space=pltpu.VMEM)
    return pl.pallas_call(
        kernel,
        out_shape=[jax.ShapeDtypeStruct(shape, jnp.float32) for shape in outs],
        in_specs=[pl.BlockSpec(memory_space=pltpu.SMEM)] + [whole] * len(arrays),
        out_specs=[whole] * len(outs),
        scratch_shapes=[pltpu.VMEM(shape, jnp.float32) for shape in scratch],
        compiler_params=pltpu.CompilerParams(vmem_limit_bytes=24 << 20),
    )(offsets, *arrays)


def shifted(x, axis, by):
    peers = lax.axis_size(axis)
    return lax.ppermute(x, axis, [(i, (i + by) % peers) for i in range(peers)])


def nearest(shift, width):
    return (shift + width // 2) // width


def to_block(rotor, blocks):
    peers = lax.axis_size("theta")
    moves = [lambda x, b=b: shifted(x, "theta", b) for b in range(peers)]
    return lax.switch(jnp.mod(blocks, peers), moves, rotor)


def exact(rotor, shift):
    peers = lax.axis_size("theta")
    width = rotor.shape[1]
    group = width // 2
    shift = jnp.mod(shift, width * peers)

    def move(total):
        blocks, rest = divmod(total * group, width)

        def run(x):
            here = shifted(x[:, : width - rest], "theta", blocks)
            before = shifted(x[:, width - rest - group + 1 :], "theta", blocks + 1)
            return jnp.concatenate([before, here], axis=1)

        return run

    return lax.switch(shift // group, [move(i) for i in range(peers * width // group)], rotor)


def swapped(inner, outer, axis, wraps):
    peers = lax.axis_size(axis)
    within = [(i, i ^ 1) for i in range(peers)]
    across = [(i, i + 1 if i % 2 else i - 1) for i in range(peers)]
    if wraps:
        outer = lax.ppermute(outer, axis, [(i, j % peers) for i, j in across])
        return lax.ppermute(inner, axis, within), outer
    inner = lax.ppermute(inner, axis, within)
    return inner, lax.ppermute(outer, axis, [(i, j) for i, j in across if 0 <= j < peers])


def pack_layers(offsets, rotor, velocity, seed_in, mask_in, inner, outer, stator, seed, mask, done):
    copies = [
        pltpu.make_async_copy(velocity.at[:, :, :, pl.ds(RB, RB)], stator, done.at[0]),
        pltpu.make_async_copy(seed_in, seed, done.at[1]),
        pltpu.make_async_copy(mask_in, mask, done.at[2]),
    ]
    for copy in copies:
        copy.start()
    for copy in copies:
        copy.wait()
    even = is_even("gz") == 1
    nz = rotor.shape[2]
    for c in range(3):
        for row in range(rotor.shape[1]):
            ends = []
            for z0, z1, z2 in ((nz - ZH, nz - 2, nz - 3 + c), (0, 0, c)):
                solid = mask[row, z2 : z2 + 1, :].astype(jnp.float32)
                blank = jnp.zeros((1, RB), jnp.float32)
                left = [rotor[c, row, z0 : z0 + ZH, :], seed[c, row, z1 : z1 + 2, :RB], solid[:, :RB], blank]
                right = [stator[c, row, z0 : z0 + ZH, :], seed[c, row, z1 : z1 + 2, RB:], solid[:, RB:], blank]
                ends.append([jnp.concatenate(left, axis=0), jnp.concatenate(right, axis=0)])
            top, bottom = ends
            for half in range(2):
                lanes = slice(half * RB, half * RB + RB)
                inner[c, row, :, lanes] = jnp.where(even, top[half], bottom[half])
                outer[c, row, :, lanes] = jnp.where(even, bottom[half], top[half])


def send_rows(h, rotor, stator, extra, inner, outer):
    width = rotor.shape[1]
    reach = width // 2 + h
    even = is_even("theta")
    for target, last in ((inner, even), (outer, 1 - even)):
        target[:, :reach] = rotor[:, pl.ds(last * (width - reach), reach)]
        target[:, reach : reach + h] = stator[:, pl.ds(last * (width - h), h)]
        if extra is not None:
            edge = extra[:, pl.ds(last * (width - 1), 1)]
            target[:, reach + h : reach + h + 1] = edge[..., :RB]
            target[:, reach + h + 1 :] = edge[..., RB:]


def unpack_layers(
    offsets, inner, outer, rotor, stator, seed, mask,
    rotor_out, stator_out, seed_out, solid_out, rows_out, rows_in,
):
    even = is_even("gz") == 1
    nz = rotor.shape[2]
    none = jnp.zeros((2, NR), jnp.float32)
    blank = jnp.zeros((1, NR), jnp.float32)
    for row in range(rotor.shape[1]):
        solid_above, solid_below = [], []
        for c in range(3):
            one, two = inner[c, row], outer[c, row]
            above, below = jnp.where(even, one, two), jnp.where(even, two, one)
            halo = jnp.concatenate([above[:ZH], below[:ZH]], axis=0)
            rotor_out[c, row, :nz, :] = rotor[c, row]
            rotor_out[c, row, nz:, :] = halo[:, :RB]
            stator_out[c, row, :nz, :] = stator[c, row]
            stator_out[c, row, nz:, :] = halo[:, RB:]
            seed_out[c, row, :nz, :] = seed[c, row]
            seed_out[c, row, nz:, :] = jnp.concatenate(
                [above[ZH : ZH + 2], none, none, below[ZH : ZH + 2]], axis=0
            )
            solid_above.append(above[ZH + 2 : ZH + 3])
            solid_below.append(below[ZH + 2 : ZH + 3])
        solid_out[row, :nz, :] = mask[row].astype(jnp.float32)
        solid_out[row, nz:, :] = jnp.concatenate(solid_above + [blank, blank] + solid_below, axis=0)
    send_rows(2, rotor_out, stator_out, seed_out, rows_in, rows_out)


def pack_rows(offsets, rotor, stator, outer, inner):
    send_rows(2, rotor, stator, None, inner, outer)


def pack_last_rows(offsets, packed, stator, outer, inner, rotor):
    _, width, layers, _ = rotor.shape
    nz = packed.shape[2]
    none = jnp.zeros((layers - nz - 2, RB), jnp.float32)
    for c in range(3):
        for row in range(width):
            rotor[c, row, :nz, :] = packed[c, row]
            beyond = packed[c, width, 2 * row : 2 * row + 2, :]
            rotor[c, row, nz:, :] = jnp.concatenate([beyond[:1], none, beyond[1:]], axis=0)
    send_rows(1, rotor, stator, None, inner, outer)


def gather(remain, h, inner, outer, rotor, stator, rotors, field):
    width = rotor.shape[1]
    reach = width // 2 + h
    even = is_even("theta")
    rotors[:, reach : reach + width] = rotor[...]
    rotors[:, pl.ds(even * (reach + width), reach)] = inner[:, :reach]
    rotors[:, pl.ds((1 - even) * (reach + width), reach)] = outer[:, :reach]
    field[..., :RB] = rotors[:, pl.ds(reach - h - remain, width + 2 * h)]
    field[:, h : h + width, :, RB:] = stator[...]
    field[:, pl.ds(even * (h + width), h), :, RB:] = inner[:, reach : reach + h]
    field[:, pl.ds((1 - even) * (h + width), h), :, RB:] = outer[:, reach : reach + h]


def multiply(rows, weight):
    flat = rows.astype(jnp.bfloat16).reshape(-1, NR)
    return rows + jnp.dot(flat, weight[...], preferred_element_type=jnp.float32).reshape(rows.shape)


def around(x, row):
    mid = x[row]
    layers = mid.shape[0]
    lane = lax.broadcasted_iota(jnp.int32, mid.shape, 1)
    rp = jnp.where(lane == NR - 1, 0.0, pltpu.roll(mid, NR - 1, 1))
    rm = jnp.where(lane == 0, 0.0, pltpu.roll(mid, 1, 1))
    return mid, x[row + 1], x[row - 1], pltpu.roll(mid, layers - 1, 0), pltpu.roll(mid, 1, 0), rp, rm


def laplace(mid, tp, tm, zp, zm, rp, rm):
    return tp + tm + zp + zm + rp + rm - 6.0 * mid


def viscosity(sides):
    total = 0.0
    for _, tp, tm, zp, zm, rp, rm in sides:
        total = total + (tp - tm) ** 2 + (zp - zm) ** 2 + (rp - rm) ** 2
    return 0.05 + 0.95 * lax.rsqrt(jnp.sqrt(1.0 + total))


def within_ends(layers):
    place = lax.broadcasted_iota(jnp.int32, (layers, NR), 0)
    nz = layers - 2 * ZH
    layer = lax.axis_index("gz") * nz + jnp.where(place >= layers - ZH, place - layers, place)
    return ((layer >= 0) & (layer < lax.axis_size("gz") * nz)).astype(jnp.float32)


def forward_first(offsets, outer, inner, rotor, stator, solid, weight, visc, u_rotor, u_stator, rotors, w):
    gather(left_over(offsets[0], rotor.shape[1]), 2, inner, outer, rotor, stator, rotors, w)
    for c in range(3):
        w[c] = multiply(w[c], weight)
    width, layers = rotor.shape[1:3]
    inside = within_ends(layers)
    for row in range(width + 2):
        sides = [around(w.at[c], row + 1) for c in range(3)]
        mu = viscosity(sides)
        visc[row] = mu
        if 1 <= row <= width:
            damp = 0.5 * solid[row - 1]
            for c in range(3):
                u = inside * (sides[c][0] + 0.1 * mu * laplace(*sides[c]) - damp * sides[c][0])
                u_rotor[c, row - 1] = u[:, :RB]
                u_stator[c, row - 1] = u[:, RB:]


def forward_last(
    offsets, outer, inner, rotor, stator, solid, weight, back_weight, seed, first_in, first_out,
    ending, lam_rotor, lam_stator, rotors, w, scaled, after,
):
    gather(left_over(offsets[1], rotor.shape[1]), 2, inner, outer, rotor, stator, rotors, w)
    for c in range(3):
        w[c] = multiply(w[c], weight)
    width, layers = rotor.shape[1:3]
    nz = layers - 2 * ZH
    even = is_even("theta") == 1
    inside = within_ends(layers)
    for row in range(width + 2):
        sides = [around(w.at[c], row + 1) for c in range(3)]
        mu = viscosity(sides)
        for c in range(3):
            if 1 <= row <= width:
                lam = seed[c, row - 1]
                scaled[c, row] = mu * lam
                mid = sides[c][0]
                u = mid + 0.1 * mu * laplace(*sides[c]) - 0.5 * solid[row - 1] * mid
                ending[c, row - 1] = u[:nz]
            else:
                one, two = (first_out, first_in) if row == 0 else (first_in, first_out)
                for half in range(2):
                    at = one.shape[1] - 2 + half
                    lam = jnp.where(even, one[c, at], two[c, at])
                    lanes = slice(half * RB, half * RB + RB)
                    scaled[c, row, :, lanes] = mu[:, lanes] * lam
    for c in range(3):
        for row in range(width):
            lam = seed[c, row]
            after[row] = lam + 0.1 * laplace(*around(scaled.at[c], row + 1)) - 0.5 * solid[row] * lam
        lam = inside * multiply(after[...], back_weight)
        lam_stator[c] = lam[..., RB:]
        lam_rotor[c, :width] = lam[:, :nz, :RB]
        for row in range(width):
            lam_rotor[c, width, 2 * row : 2 * row + 1, :] = lam[row, nz : nz + 1, :RB]
            lam_rotor[c, width, 2 * row + 1 : 2 * row + 2, :] = lam[row, layers - 1 :, :RB]


def adjoint_first(
    offsets, outer, inner, rotor, stator, solid, back_weight, visc, b_rotor, b_stator, rotors, lam, scaled, after
):
    gather(left_over(-offsets[1], rotor.shape[1]), 1, inner, outer, rotor, stator, rotors, lam)
    width, layers = rotor.shape[1:3]
    nz = layers - 2 * ZH
    for c in range(3):
        scaled[c] = visc[...] * lam[c]
        for row in range(width):
            mid = lam[c, row + 1]
            a = mid + 0.1 * laplace(*around(scaled.at[c], row + 1)) - 0.5 * solid[row] * mid
            after[row] = a[:nz]
        b = multiply(after[...], back_weight)
        b_rotor[c] = b[..., :RB]
        b_stator[c] = b[..., RB:]


def join(offsets, rows, stator, out):
    width = stator.shape[1]
    group = width // 2
    out[..., :RB] = rows[:, pl.ds(group - 1 - (-offsets[0] & (group - 1)), width)]
    out[..., RB:] = stator[...]


def load(offsets, rotor, velocity, seed, mask):
    _, width, nz, _ = velocity.shape
    edge = jax.ShapeDtypeStruct((3, width, 2 * ZH, NR), jnp.float32)
    whole = pl.BlockSpec(memory_space=pltpu.VMEM)
    far = pl.BlockSpec(memory_space=pl.ANY)
    return pl.pallas_call(
        pack_layers,
        out_shape=[
            edge,
            edge,
            jax.ShapeDtypeStruct((3, width, nz, RB), jnp.float32),
            jax.ShapeDtypeStruct(seed.shape, jnp.float32),
            jax.ShapeDtypeStruct(mask.shape, jnp.int32),
        ],
        in_specs=[pl.BlockSpec(memory_space=pltpu.SMEM), whole, far, far, far],
        out_specs=[whole] * 5,
        scratch_shapes=[pltpu.SemaphoreType.DMA((3,))],
        compiler_params=pltpu.CompilerParams(vmem_limit_bytes=24 << 20),
    )(offsets, rotor, velocity, seed, mask)


def body(velocity, adjoint_seed, rotor_offset, design_mask, interface_band_weight):
    _, width, nz, _ = velocity.shape
    zs = nz + 2 * ZH
    spread = jnp.pad(interface_band_weight, ((0, 0), (LOWER, NR - UPPER)))
    back_weight = jnp.pad(interface_band_weight.T, ((LOWER, NR - UPPER), (0, 0)))
    blocks0 = nearest(rotor_offset[0], width)
    blocks1 = nearest(rotor_offset[1], width)
    back1 = nearest(-rotor_offset[1], width)
    group = width // 2
    block = (3, width, zs, RB)

    def ext(rows):
        return (3, rows, zs, RB)

    rotor = to_block(velocity[..., :RB], blocks0)
    inner, outer, stator, seed, mask = load(rotor_offset, rotor, velocity, adjoint_seed, design_mask)
    inner, outer = swapped(inner, outer, "gz", False)
    rotor, stator, seed, solid, outer, inner = call(
        unpack_layers,
        [block, block, (3, width, zs, NR), (width, zs, NR), ext(group + 6), ext(group + 6)],
        rotor_offset, inner, outer, rotor, stator, seed, mask,
    )
    first_in, first_out = swapped(inner, outer, "theta", True)
    visc, rotor, stator = call(
        forward_first,
        [(width + 2, zs, NR), block, block],
        rotor_offset, first_out, first_in, rotor, stator, solid, spread,
        scratch=[ext(2 * width + 4), (3, width + 4, zs, NR)],
    )

    rotor = to_block(rotor, blocks1)
    outer, inner = call(pack_rows, [ext(group + 4)] * 2, rotor_offset, rotor, stator)
    inner, outer = swapped(inner, outer, "theta", True)
    ending, rotor, stator = call(
        forward_last,
        [(3, width, nz, NR), (3, width + 1, nz, RB), block],
        rotor_offset, outer, inner, rotor, stator, solid, spread, back_weight, seed, first_in, first_out,
        scratch=[ext(2 * width + 4), (3, width + 4, zs, NR), (3, width + 2, zs, NR), (width, zs, NR)],
    )

    rotor = to_block(rotor, back1)
    outer, inner, rotor = call(pack_last_rows, [ext(group + 2)] * 2 + [block], rotor_offset, rotor, stator)
    inner, outer = swapped(inner, outer, "theta", True)
    rotor, stator = call(
        adjoint_first,
        [(3, width, nz, RB)] * 2,
        rotor_offset, outer, inner, rotor, stator, solid, back_weight, visc,
        scratch=[ext(2 * width + 2), (3, width + 2, zs, NR), (3, width + 2, zs, NR), (width, nz, NR)],
    )
    rows = exact(rotor, -rotor_offset[0])
    (adjoint,) = call(join, [(3, width, nz, NR)], rotor_offset, rows, stator)
    return ending, adjoint


def solution(mesh):
    return jax.shard_map(
        body,
        mesh=mesh,
        in_specs=(
            P(None, "theta", "gz", None),
            P(None, "theta", "gz", None),
            P(),
            P("theta", "gz", None),
            P(),
        ),
        out_specs=(P(None, "theta", "gz", None), P(None, "theta", "gz", None)),
        check_vma=False,
    )
```

time: 130 us -> 140 us (1.077)
  the two profiles are of different devices: /device:TPU:29 before, /device:TPU:31 now
where the time goes in v2:
time: 140 us; the launch traced here: 139 us
  starting transfers between devices  65 us (46%)
  waiting for transfers between devices  52.5 us (38%)
  Pallas kernels  11.3 us (8%)
  local copies, waits for them, and re-layouts  5.74 us (4%)
  between operations  4.19 us (3%)
    ppermute x5, waiting for transfers between devices, shifted(): return lax.ppermute(x, axis, [(i, (i + by) % peers) for i in range(peers)])  44.6 us
    ppermute x5, starting transfers between devices, shifted(): return lax.ppermute(x, axis, [(i, (i + by) % peers) for i in range(peers)])  30.6 us
    ppermute x3, starting transfers between devices, swapped(): return (lax.ppermute(inner, axis, within), outer)  13.5 us
    ppermute x3, starting transfers between devices, swapped(): outer = lax.ppermute(outer, axis, [(i, j % peers) for i, j in across])  11.9 us
    pallas_call x7, Pallas kernels, call(): pl.pallas_call(kernel, out_shape=[jax.ShapeDtypeStruct(shape, jnp.float32...  9.9 us
    ppermute x1, starting transfers between devices, swapped(): lax.ppermute(outer, axis, [(i, j) for i, j in across if 0 <= j < peers])  5.98 us
    ppermute x1, waiting for transfers between devices, swapped(): lax.ppermute(outer, axis, [(i, j) for i, j in across if 0 <= j < peers])  4.83 us
    unnamed x11, local copies, waits for them, and re-layouts  3.35 us
  transfers between devices with their start and end apart: 13, of which 9 were waited for; matrix products, arithmetic and copies ran while one was open for 0% of the time, Pallas kernels for 0%

profile of v2, /device:TPU:31, one launch (start us, length us, event | category | flops | bytes accessed | tf_op | source)
XLA Modules:
  0.0 139.0 jit_solution(2949229210426928711)
XLA Ops:
  0.6 1.3 fusion
  3.6 18.1 %conditional.4 = (f32[3,8,16,128]{3,2,1,0:T(8,128)}) conditional(s32[]{:T(128)} %clamp.13, f32[3,8,16,128]{3,2,1,0:T(8,128)S(1)} %slice.397, f32[3,8,16,128]{3,2,1,0:T(8,128)S(1)} %slice.397, f32[3,8,16,128]{3,2,1,0:T(8,128)S(1)} %slice.397, f32[3,8,16,128]{3,2,1,0:T(8,128)S(1)} %slice.397, ...), branch_computations={%region_0.1_spmd, %region_1.2_spmd, %region_2.3_spmd, %region_3.4_... | conditional | bytes 786480 | solution.py:50
  3.6 11.2 %collective-permute-start.13 = (f32[3,8,16,128]{3,2,1,0:T(8,128)S(1)}, f32[3,8,16,128]{3,2,1,0:T(8,128)}, u32[]{:S(2)}, u32[]{:S(2)}) collective-permute-start(f32[3,8,16,128]{3,2,1,0:T(8,128)S(1)} %param.13), channel_id=1, source_target_pairs={{0,208},{16,224},{32,240},{48,256},{64,272},{80,288},{96,304},{112... | collective-permute-start | bytes 589832 | tf_op jit(solution)/shard_map/cond/branch_13_fun/ppermute | solution.py:40
  14.9 6.8 %collective-permute-done.13 = f32[3,8,16,128]{3,2,1,0:T(8,128)} collective-permute-done((f32[3,8,16,128]{3,2,1,0:T(8,128)S(1)}, f32[3,8,16,128]{3,2,1,0:T(8,128)}, u32[]{:S(2)}, u32[]{:S(2)}) %collective-permute-start.13) | collective-permute-done | bytes 196640 | tf_op jit(solution)/shard_map/cond/branch_13_fun/ppermute | solution.py:40
  24.2 1.4 %shard_map.68 = (f32[3,8,8,256]{3,2,1,0:T(8,128)S(1)}, f32[3,8,8,256]{3,2,1,0:T(8,128)S(1)}, f32[3,8,16,128]{3,2,1,0:T(8,128)S(1)}, f32[3,8,16,256]{3,2,1,0:T(8,128)S(1)}, s32[8,16,256]{2,1,0:T(8,128)S(1)}) custom-call(s32[2]{0:T(128)S(1)} %copy-done.3, f32[3,8,16,128]{3,2,1,0:T(8,128)} %get-tuple-element.376.rotor, f32[3,8,16,256]{3,2,1,0:T(8,128)S(1)} %copy-done, ...), custom_call_target="tpu_custom_call" | custom-call | tf_op jit(solution)/shard_map/pallas_call | solution.py:301
  25.7 3.0 %collective-permute-start.224 = (f32[3,8,8,256]{3,2,1,0:T(8,128)S(1)}, f32[3,8,8,256]{3,2,1,0:T(8,128)S(1)}, u32[]{:S(2)}, u32[]{:S(2)}) collective-permute-start(f32[3,8,8,256]{3,2,1,0:T(8,128)S(1)} %get-tuple-element.350), channel_id=1, source_target_pairs={{0,1},{1,0},{2,3},{3,2},{4,5},{5,4},{6,7},{7,6},{8,9},{9,8},{10,11... | collective-permute-start | bytes 589832 | tf_op jit(solution)/shard_map/ppermute | solution.py:79
  28.7 6.0 %collective-permute-start.225 = (f32[3,8,8,256]{3,2,1,0:T(8,128)S(1)}, f32[3,8,8,256]{3,2,1,0:T(8,128)S(1)}, u32[]{:S(2)}, u32[]{:S(2)}) collective-permute-start(f32[3,8,8,256]{3,2,1,0:T(8,128)S(1)} %get-tuple-element.351), channel_id=1, source_target_pairs={{1,2},{2,1},{3,4},{4,3},{5,6},{6,5},{7,8},{8,7},{9,10},{10,9},{11,... | collective-permute-start | bytes 589832 | tf_op jit(solution)/shard_map/ppermute | solution.py:80
  35.1 4.8 %collective-permute-done.225.outer = f32[3,8,8,256]{3,2,1,0:T(8,128)S(1)} collective-permute-done((f32[3,8,8,256]{3,2,1,0:T(8,128)S(1)}, f32[3,8,8,256]{3,2,1,0:T(8,128)S(1)}, u32[]{:S(2)}, u32[]{:S(2)}) %collective-permute-start.225) | collective-permute-done | bytes 196640 | tf_op jit(solution)/shard_map/ppermute | solution.py:80
  40.0 1.1 shard_map.69
  41.1 1.9 %collective-permute-start.226 = (f32[3,10,24,128]{3,2,1,0:T(8,128)S(1)}, f32[3,10,24,128]{3,2,1,0:T(8,128)S(1)}, u32[]{:S(2)}, u32[]{:S(2)}) collective-permute-start(f32[3,10,24,128]{3,2,1,0:T(8,128)S(1)} %get-tuple-element.355), channel_id=1, source_target_pairs={{0,496},{16,32},{32,16},{48,64},{64,48},{80,96},{96,80},{112,128},... | collective-permute-start | bytes 1105928 | tf_op jit(solution)/shard_map/ppermute | solution.py:77
  43.0 3.5 %collective-permute-start.227 = (f32[3,10,24,128]{3,2,1,0:T(8,128)S(1)}, f32[3,10,24,128]{3,2,1,0:T(8,128)S(1)}, u32[]{:S(2)}, u32[]{:S(2)}) collective-permute-start(f32[3,10,24,128]{3,2,1,0:T(8,128)S(1)} %get-tuple-element.356), channel_id=1, source_target_pairs={{0,16},{16,0},{32,48},{48,32},{64,80},{80,64},{96,112},{112,96},{1... | collective-permute-start | bytes 1105928 | tf_op jit(solution)/shard_map/ppermute | solution.py:78
  48.1 2.1 %collective-permute-done.226.outer.first_out = f32[3,10,24,128]{3,2,1,0:T(8,128)S(1)} collective-permute-done((f32[3,10,24,128]{3,2,1,0:T(8,128)S(1)}, f32[3,10,24,128]{3,2,1,0:T(8,128)S(1)}, u32[]{:S(2)}, u32[]{:S(2)}) %collective-permute-start.226) | collective-permute-done | bytes 368672 | tf_op jit(solution)/shard_map/ppermute | solution.py:77
  50.2 1.6 %shard_map.70 = (f32[10,24,256]{2,1,0:T(8,128)S(1)}, f32[3,8,24,128]{3,2,1,0:T(8,128)S(1)}, f32[3,8,24,128]{3,2,1,0:T(8,128)S(1)}) custom-call(s32[2]{0:T(128)S(1)} %copy-done.3, f32[3,10,24,128]{3,2,1,0:T(8,128)S(1)} %collective-permute-done.226.outer.first_out, f32[3,10,24,128]{3,2,1,0:T(8,128)S(1)} %collective-permute-done.227.inner.first_in, ...), custom_call_target="tpu_custom_call" | custom-call | tf_op jit(solution)/shard_map/pallas_call | solution.py:28
  51.8 21.8 %conditional.5 = (f32[3,8,24,128]{3,2,1,0:T(8,128)}) conditional(s32[]{:T(128)} %clamp.12, f32[3,8,24,128]{3,2,1,0:T(8,128)S(1)} %get-tuple-element.360, f32[3,8,24,128]{3,2,1,0:T(8,128)S(1)} %get-tuple-element.360, f32[3,8,24,128]{3,2,1,0:T(8,128)S(1)} %get-tuple-element.360, ...), branch_computations={%region_32.33_spmd, %region_33.34_spmd, %region_34.35_spmd, %regio... | conditional | bytes 1179696 | solution.py:50
  51.8 3.3 %collective-permute-start.58 = (f32[3,8,24,128]{3,2,1,0:T(8,128)S(1)}, f32[3,8,24,128]{3,2,1,0:T(8,128)}, u32[]{:S(2)}, u32[]{:S(2)}) collective-permute-start(f32[3,8,24,128]{3,2,1,0:T(8,128)S(1)} %param.58), channel_id=1, source_target_pairs={{0,416},{16,432},{32,448},{48,464},{64,480},{80,496},{96,0},{112,1... | collective-permute-start | bytes 884744 | tf_op jit(solution)/shard_map/cond/branch_26_fun/ppermute | solution.py:40
  55.1 18.4 %collective-permute-done.58 = f32[3,8,24,128]{3,2,1,0:T(8,128)} collective-permute-done((f32[3,8,24,128]{3,2,1,0:T(8,128)S(1)}, f32[3,8,24,128]{3,2,1,0:T(8,128)}, u32[]{:S(2)}, u32[]{:S(2)}) %collective-permute-start.58) | collective-permute-done | bytes 294944 | tf_op jit(solution)/shard_map/cond/branch_26_fun/ppermute | solution.py:40
  73.6 1.0 shard_map.71
  74.6 6.3 %collective-permute-start.228 = (f32[3,8,24,128]{3,2,1,0:T(8,128)S(1)}, f32[3,8,24,128]{3,2,1,0:T(8,128)S(1)}, u32[]{:S(2)}, u32[]{:S(2)}) collective-permute-start(f32[3,8,24,128]{3,2,1,0:T(8,128)S(1)} %get-tuple-element.362), channel_id=1, source_target_pairs={{0,496},{16,32},{32,16},{48,64},{64,48},{80,96},{96,80},{112,128},... | collective-permute-start | bytes 884744 | tf_op jit(solution)/shard_map/ppermute | solution.py:77
  80.9 3.9 %collective-permute-start.229 = (f32[3,8,24,128]{3,2,1,0:T(8,128)S(1)}, f32[3,8,24,128]{3,2,1,0:T(8,128)S(1)}, u32[]{:S(2)}, u32[]{:S(2)}) collective-permute-start(f32[3,8,24,128]{3,2,1,0:T(8,128)S(1)} %get-tuple-element.363), channel_id=1, source_target_pairs={{0,16},{16,0},{32,48},{48,32},{64,80},{80,64},{96,112},{112,96},{1... | collective-permute-start | bytes 884744 | tf_op jit(solution)/shard_map/ppermute | solution.py:78
  85.9 2.8 %shard_map.72 = (f32[3,8,16,256]{3,2,1,0:T(8,128)}, f32[3,9,16,128]{3,2,1,0:T(8,128)S(1)}, f32[3,8,24,128]{3,2,1,0:T(8,128)S(1)}) custom-call(s32[2]{0:T(128)S(1)} %copy-done.3, f32[3,8,24,128]{3,2,1,0:T(8,128)S(1)} %collective-permute-done.228.outer, f32[3,8,24,128]{3,2,1,0:T(8,128)S(1)} %collective-permute-done.229.inner, ...), custom_call_target="tpu_custom_call" | custom-call | tf_op jit(solution)/shard_map/pallas_call | solution.py:28
  88.8 17.8 %conditional.6 = (f32[3,9,16,128]{3,2,1,0:T(8,128)}) conditional(s32[]{:T(128)} %clamp.15, f32[3,9,16,128]{3,2,1,0:T(8,128)S(1)} %get-tuple-element.366, f32[3,9,16,128]{3,2,1,0:T(8,128)S(1)} %get-tuple-element.366, f32[3,9,16,128]{3,2,1,0:T(8,128)S(1)} %get-tuple-element.366, ...), branch_computations={%region_64.65_spmd, %region_65.66_spmd, %region_66.67_spmd, %regio... | conditional | bytes 884784 | solution.py:50
  88.8 7.4 %collective-permute-start.71 = (f32[3,9,16,128]{3,2,1,0:T(8,128)S(1)}, f32[3,9,16,128]{3,2,1,0:T(8,128)}, u32[]{:S(2)}, u32[]{:S(2)}) collective-permute-start(f32[3,9,16,128]{3,2,1,0:T(8,128)S(1)} %param.71), channel_id=1, source_target_pairs={{0,112},{16,128},{32,144},{48,160},{64,176},{80,192},{96,208},{112... | collective-permute-start | bytes 663560 | tf_op jit(solution)/shard_map/cond/branch_7_fun/ppermute | solution.py:40
  96.2 10.4 %collective-permute-done.71 = f32[3,9,16,128]{3,2,1,0:T(8,128)} collective-permute-done((f32[3,9,16,128]{3,2,1,0:T(8,128)S(1)}, f32[3,9,16,128]{3,2,1,0:T(8,128)}, u32[]{:S(2)}, u32[]{:S(2)}) %collective-permute-start.71) | collective-permute-done | bytes 221216 | tf_op jit(solution)/shard_map/cond/branch_7_fun/ppermute | solution.py:40
  106.6 1.0 shard_map.73
  107.6 3.7 %collective-permute-start.230 = (f32[3,6,24,128]{3,2,1,0:T(8,128)S(1)}, f32[3,6,24,128]{3,2,1,0:T(8,128)S(1)}, u32[]{:S(2)}, u32[]{:S(2)}) collective-permute-start(f32[3,6,24,128]{3,2,1,0:T(8,128)S(1)} %get-tuple-element.368), channel_id=1, source_target_pairs={{0,496},{16,32},{32,16},{48,64},{64,48},{80,96},{96,80},{112,128},... | collective-permute-start | bytes 663560 | tf_op jit(solution)/shard_map/ppermute | solution.py:77
  111.2 6.2 %collective-permute-start.231 = (f32[3,6,24,128]{3,2,1,0:T(8,128)S(1)}, f32[3,6,24,128]{3,2,1,0:T(8,128)S(1)}, u32[]{:S(2)}, u32[]{:S(2)}) collective-permute-start(f32[3,6,24,128]{3,2,1,0:T(8,128)S(1)} %get-tuple-element.369), channel_id=1, source_target_pairs={{0,16},{16,0},{32,48},{48,32},{64,80},{80,64},{96,112},{112,96},{1... | collective-permute-start | bytes 663560 | tf_op jit(solution)/shard_map/ppermute | solution.py:78
  118.8 1.1 shard_map.74
  119.9 17.8 %conditional.7 = (f32[3,11,16,128]{3,2,1,0:T(8,128)S(1)}) conditional(s32[]{:T(128)} %clamp.14, f32[3,8,16,128]{3,2,1,0:T(8,128)S(1)} %get-tuple-element.372, f32[3,8,16,128]{3,2,1,0:T(8,128)S(1)} %get-tuple-element.372, f32[3,8,16,128]{3,2,1,0:T(8,128)S(1)} %get-tuple-element.372, ...), branch_computations={%region_96.97_spmd, %region_97.98_spmd, %region_98.99_spmd, %regio... | conditional | flops 67584 | bytes 2162776 | solution.py:69
  119.9 1.9 %collective-permute-start.173 = (f32[3,8,16,128]{3,2,1,0:T(8,128)S(1)}, f32[3,8,16,128]{3,2,1,0:T(8,128)S(1)}, u32[]{:S(2)}, u32[]{:S(2)}) collective-permute-start(f32[3,8,16,128]{3,2,1,0:T(8,128)S(1)} %param.134), channel_id=1, source_target_pairs={{0,304},{16,320},{32,336},{48,352},{64,368},{80,384},{96,400},{112... | collective-permute-start | bytes 589832 | tf_op jit(solution)/shard_map/cond/branch_38_fun/ppermute | solution.py:40
  121.9 6.7 %collective-permute-start.172 = (f32[3,3,16,128]{3,2,1,0:T(8,128)S(1)}, f32[3,3,16,128]{3,2,1,0:T(8,128)S(1)}, u32[]{:S(2)}, u32[]{:S(2)}) collective-permute-start(f32[3,3,16,128]{3,2,1,0:T(8,128)S(1)} %slice.353), channel_id=1, source_target_pairs={{0,320},{16,336},{32,352},{48,368},{64,384},{80,400},{96,416},{112... | collective-permute-start | bytes 221192 | tf_op jit(solution)/shard_map/cond/branch_38_fun/ppermute | solution.py:40
  128.6 9.0 %collective-permute-done.172 = f32[3,3,16,128]{3,2,1,0:T(8,128)S(1)} collective-permute-done((f32[3,3,16,128]{3,2,1,0:T(8,128)S(1)}, f32[3,3,16,128]{3,2,1,0:T(8,128)S(1)}, u32[]{:S(2)}, u32[]{:S(2)}) %collective-permute-start.172) | collective-permute-done | bytes 73760 | tf_op jit(solution)/shard_map/cond/branch_38_fun/ppermute | solution.py:40
  137.7 1.3 shard_map.75
  (23 shorter events, 5.4 us)
Async XLA Ops:
  0.6 21.0 %copy-start = (f32[3,8,16,256]{3,2,1,0:T(8,128)S(1)}, f32[3,8,16,256]{3,2,1,0:T(8,128)}, u32[]{:S(2)}) copy-start(f32[3,8,16,256]{3,2,1,0:T(8,128)} %velocity.1) | copy-start | bytes 1179652
  3.6 18.0 %collective-permute-start.13 = (f32[3,8,16,128]{3,2,1,0:T(8,128)S(1)}, f32[3,8,16,128]{3,2,1,0:T(8,128)}, u32[]{:S(2)}, u32[]{:S(2)}) collective-permute-start(f32[3,8,16,128]{3,2,1,0:T(8,128)S(1)} %param.13), channel_id=1, source_target_pairs={{0,208},{16,224},{32,240},{48,256},{64,272},{80,288},{96,304},{112... | collective-permute-start | bytes 589832 | tf_op jit(solution)/shard_map/cond/branch_13_fun/ppermute | solution.py:40
  21.7 0.7 copy-start.3
  22.3 1.0 copy-start.1
  23.3 0.9 copy-start.2
  25.7 9.5 %collective-permute-start.224 = (f32[3,8,8,256]{3,2,1,0:T(8,128)S(1)}, f32[3,8,8,256]{3,2,1,0:T(8,128)S(1)}, u32[]{:S(2)}, u32[]{:S(2)}) collective-permute-start(f32[3,8,8,256]{3,2,1,0:T(8,128)S(1)} %get-tuple-element.350), channel_id=1, source_target_pairs={{0,1},{1,0},{2,3},{3,2},{4,5},{5,4},{6,7},{7,6},{8,9},{9,8},{10,11... | collective-permute-start | bytes 589832 | tf_op jit(solution)/shard_map/ppermute | solution.py:79
  28.7 11.3 %collective-permute-start.225 = (f32[3,8,8,256]{3,2,1,0:T(8,128)S(1)}, f32[3,8,8,256]{3,2,1,0:T(8,128)S(1)}, u32[]{:S(2)}, u32[]{:S(2)}) collective-permute-start(f32[3,8,8,256]{3,2,1,0:T(8,128)S(1)} %get-tuple-element.351), channel_id=1, source_target_pairs={{1,2},{2,1},{3,4},{4,3},{5,6},{6,5},{7,8},{8,7},{9,10},{10,9},{11,... | collective-permute-start | bytes 589832 | tf_op jit(solution)/shard_map/ppermute | solution.py:80
  41.1 9.1 %collective-permute-start.226 = (f32[3,10,24,128]{3,2,1,0:T(8,128)S(1)}, f32[3,10,24,128]{3,2,1,0:T(8,128)S(1)}, u32[]{:S(2)}, u32[]{:S(2)}) collective-permute-start(f32[3,10,24,128]{3,2,1,0:T(8,128)S(1)} %get-tuple-element.355), channel_id=1, source_target_pairs={{0,496},{16,32},{32,16},{48,64},{64,48},{80,96},{96,80},{112,128},... | collective-permute-start | bytes 1105928 | tf_op jit(solution)/shard_map/ppermute | solution.py:77
  43.0 7.2 %collective-permute-start.227 = (f32[3,10,24,128]{3,2,1,0:T(8,128)S(1)}, f32[3,10,24,128]{3,2,1,0:T(8,128)S(1)}, u32[]{:S(2)}, u32[]{:S(2)}) collective-permute-start(f32[3,10,24,128]{3,2,1,0:T(8,128)S(1)} %get-tuple-element.356), channel_id=1, source_target_pairs={{0,16},{16,0},{32,48},{48,32},{64,80},{80,64},{96,112},{112,96},{1... | collective-permute-start | bytes 1105928 | tf_op jit(solution)/shard_map/ppermute | solution.py:78
  47.2 0.7 copy-start.4
  51.8 21.8 %collective-permute-start.58 = (f32[3,8,24,128]{3,2,1,0:T(8,128)S(1)}, f32[3,8,24,128]{3,2,1,0:T(8,128)}, u32[]{:S(2)}, u32[]{:S(2)}) collective-permute-start(f32[3,8,24,128]{3,2,1,0:T(8,128)S(1)} %param.58), channel_id=1, source_target_pairs={{0,416},{16,432},{32,448},{48,464},{64,480},{80,496},{96,0},{112,1... | collective-permute-start | bytes 884744 | tf_op jit(solution)/shard_map/cond/branch_26_fun/ppermute | solution.py:40
  74.6 11.0 %collective-permute-start.228 = (f32[3,8,24,128]{3,2,1,0:T(8,128)S(1)}, f32[3,8,24,128]{3,2,1,0:T(8,128)S(1)}, u32[]{:S(2)}, u32[]{:S(2)}) collective-permute-start(f32[3,8,24,128]{3,2,1,0:T(8,128)S(1)} %get-tuple-element.362), channel_id=1, source_target_pairs={{0,496},{16,32},{32,16},{48,64},{64,48},{80,96},{96,80},{112,128},... | collective-permute-start | bytes 884744 | tf_op jit(solution)/shard_map/ppermute | solution.py:77
  80.9 5.1 %collective-permute-start.229 = (f32[3,8,24,128]{3,2,1,0:T(8,128)S(1)}, f32[3,8,24,128]{3,2,1,0:T(8,128)S(1)}, u32[]{:S(2)}, u32[]{:S(2)}) collective-permute-start(f32[3,8,24,128]{3,2,1,0:T(8,128)S(1)} %get-tuple-element.363), channel_id=1, source_target_pairs={{0,16},{16,0},{32,48},{48,32},{64,80},{80,64},{96,112},{112,96},{1... | collective-permute-start | bytes 884744 | tf_op jit(solution)/shard_map/ppermute | solution.py:78
  88.8 17.8 %collective-permute-start.71 = (f32[3,9,16,128]{3,2,1,0:T(8,128)S(1)}, f32[3,9,16,128]{3,2,1,0:T(8,128)}, u32[]{:S(2)}, u32[]{:S(2)}) collective-permute-start(f32[3,9,16,128]{3,2,1,0:T(8,128)S(1)} %param.71), channel_id=1, source_target_pairs={{0,112},{16,128},{32,144},{48,160},{64,176},{80,192},{96,208},{112... | collective-permute-start | bytes 663560 | tf_op jit(solution)/shard_map/cond/branch_7_fun/ppermute | solution.py:40
  107.6 11.3 %collective-permute-start.230 = (f32[3,6,24,128]{3,2,1,0:T(8,128)S(1)}, f32[3,6,24,128]{3,2,1,0:T(8,128)S(1)}, u32[]{:S(2)}, u32[]{:S(2)}) collective-permute-start(f32[3,6,24,128]{3,2,1,0:T(8,128)S(1)} %get-tuple-element.368), channel_id=1, source_target_pairs={{0,496},{16,32},{32,16},{48,64},{64,48},{80,96},{96,80},{112,128},... | collective-permute-start | bytes 663560 | tf_op jit(solution)/shard_map/ppermute | solution.py:77
  111.2 7.6 %collective-permute-start.231 = (f32[3,6,24,128]{3,2,1,0:T(8,128)S(1)}, f32[3,6,24,128]{3,2,1,0:T(8,128)S(1)}, u32[]{:S(2)}, u32[]{:S(2)}) collective-permute-start(f32[3,6,24,128]{3,2,1,0:T(8,128)S(1)} %get-tuple-element.369), channel_id=1, source_target_pairs={{0,16},{16,0},{32,48},{48,32},{64,80},{80,64},{96,112},{112,96},{1... | collective-permute-start | bytes 663560 | tf_op jit(solution)/shard_map/ppermute | solution.py:78
  119.9 17.7 %collective-permute-start.173 = (f32[3,8,16,128]{3,2,1,0:T(8,128)S(1)}, f32[3,8,16,128]{3,2,1,0:T(8,128)S(1)}, u32[]{:S(2)}, u32[]{:S(2)}) collective-permute-start(f32[3,8,16,128]{3,2,1,0:T(8,128)S(1)} %param.134), channel_id=1, source_target_pairs={{0,304},{16,320},{32,336},{48,352},{64,368},{80,384},{96,400},{112... | collective-permute-start | bytes 589832 | tf_op jit(solution)/shard_map/cond/branch_38_fun/ppermute | solution.py:40
  121.9 15.7 %collective-permute-start.172 = (f32[3,3,16,128]{3,2,1,0:T(8,128)S(1)}, f32[3,3,16,128]{3,2,1,0:T(8,128)S(1)}, u32[]{:S(2)}, u32[]{:S(2)}) collective-permute-start(f32[3,3,16,128]{3,2,1,0:T(8,128)S(1)} %slice.353), channel_id=1, source_target_pairs={{0,320},{16,336},{32,352},{48,368},{64,384},{80,400},{96,416},{112... | collective-permute-start | bytes 221192 | tf_op jit(solution)/shard_map/cond/branch_38_fun/ppermute | solution.py:40

commit v3 on v2

--- a/solution.py
+++ b/solution.py
@@ -25,14 +25,15 @@
 
 def call(kernel, outs, offsets, *arrays, scratch=()):
     whole = pl.BlockSpec(memory_space=pltpu.VMEM)
+    numbers = [] if offsets is None else [offsets]
     return pl.pallas_call(
         kernel,
         out_shape=[jax.ShapeDtypeStruct(shape, jnp.float32) for shape in outs],
-        in_specs=[pl.BlockSpec(memory_space=pltpu.SMEM)] + [whole] * len(arrays),
+        in_specs=[pl.BlockSpec(memory_space=pltpu.SMEM)] * len(numbers) + [whole] * len(arrays),
         out_specs=[whole] * len(outs),
         scratch_shapes=[pltpu.VMEM(shape, jnp.float32) for shape in scratch],
         compiler_params=pltpu.CompilerParams(vmem_limit_bytes=24 << 20),
-    )(offsets, *arrays)
+    )(*numbers, *arrays)
 
 
 def shifted(x, axis, by):
@@ -80,7 +81,7 @@
     return inner, lax.ppermute(outer, axis, [(i, j) for i, j in across if 0 <= j < peers])
 
 
-def pack_layers(offsets, rotor, velocity, seed_in, mask_in, inner, outer, stator, seed, mask, done):
+def pack_layers(rotor, velocity, seed_in, mask_in, inner, outer, stator, seed, mask, done):
     copies = [
         pltpu.make_async_copy(velocity.at[:, :, :, pl.ds(RB, RB)], stator, done.at[0]),
         pltpu.make_async_copy(seed_in, seed, done.at[1]),
@@ -122,7 +123,7 @@
 
 
 def unpack_layers(
-    offsets, inner, outer, rotor, stator, seed, mask,
+    inner, outer, rotor, stator, seed, mask,
     rotor_out, stator_out, seed_out, solid_out, rows_out, rows_in,
 ):
     even = is_even("gz") == 1
@@ -150,11 +151,11 @@
     send_rows(2, rotor_out, stator_out, seed_out, rows_in, rows_out)
 
 
-def pack_rows(offsets, rotor, stator, outer, inner):
+def pack_rows(rotor, stator, outer, inner):
     send_rows(2, rotor, stator, None, inner, outer)
 
 
-def pack_last_rows(offsets, packed, stator, outer, inner, rotor):
+def pack_last_rows(packed, stator, outer, inner, rotor):
     _, width, layers, _ = rotor.shape
     nz = packed.shape[2]
     none = jnp.zeros((layers - nz - 2, RB), jnp.float32)
@@ -293,7 +294,7 @@
     out[..., RB:] = stator[...]
 
 
-def load(offsets, rotor, velocity, seed, mask):
+def load(rotor, velocity, seed, mask):
     _, width, nz, _ = velocity.shape
     edge = jax.ShapeDtypeStruct((3, width, 2 * ZH, NR), jnp.float32)
     whole = pl.BlockSpec(memory_space=pltpu.VMEM)
@@ -307,11 +308,11 @@
             jax.ShapeDtypeStruct(seed.shape, jnp.float32),
             jax.ShapeDtypeStruct(mask.shape, jnp.int32),
         ],
-        in_specs=[pl.BlockSpec(memory_space=pltpu.SMEM), whole, far, far, far],
+        in_specs=[whole, far, far, far],
         out_specs=[whole] * 5,
         scratch_shapes=[pltpu.SemaphoreType.DMA((3,))],
         compiler_params=pltpu.CompilerParams(vmem_limit_bytes=24 << 20),
-    )(offsets, rotor, velocity, seed, mask)
+    )(rotor, velocity, seed, mask)
 
 
 def body(velocity, adjoint_seed, rotor_offset, design_mask, interface_band_weight):
@@ -329,12 +330,12 @@
         return (3, rows, zs, RB)
 
     rotor = to_block(velocity[..., :RB], blocks0)
-    inner, outer, stator, seed, mask = load(rotor_offset, rotor, velocity, adjoint_seed, design_mask)
+    inner, outer, stator, seed, mask = load(rotor, velocity, adjoint_seed, design_mask)
     inner, outer = swapped(inner, outer, "gz", False)
     rotor, stator, seed, solid, outer, inner = call(
         unpack_layers,
         [block, block, (3, width, zs, NR), (width, zs, NR), ext(group + 6), ext(group + 6)],
-        rotor_offset, inner, outer, rotor, stator, seed, mask,
+        None, inner, outer, rotor, stator, seed, mask,
     )
     first_in, first_out = swapped(inner, outer, "theta", True)
     visc, rotor, stator = call(
@@ -345,7 +346,7 @@
     )
 
     rotor = to_block(rotor, blocks1)
-    outer, inner = call(pack_rows, [ext(group + 4)] * 2, rotor_offset, rotor, stator)
+    outer, inner = call(pack_rows, [ext(group + 4)] * 2, None, rotor, stator)
     inner, outer = swapped(inner, outer, "theta", True)
     ending, rotor, stator = call(
         forward_last,
@@ -355,7 +356,7 @@
     )
 
     rotor = to_block(rotor, back1)
-    outer, inner, rotor = call(pack_last_rows, [ext(group + 2)] * 2 + [block], rotor_offset, rotor, stator)
+    outer, inner, rotor = call(pack_last_rows, [ext(group + 2)] * 2 + [block], None, rotor, stator)
     inner, outer = swapped(inner, outer, "theta", True)
     rotor, stator = call(
         adjoint_first,

time: 140 us -> 110 us (0.79)
  the two profiles are of different devices: /device:TPU:31 before, /device:TPU:33 now
where the time goes in v3:
time: 110 us
  starting transfers between devices  54.6 us (50%)
  waiting for transfers between devices  33.7 us (31%)
  Pallas kernels  11.3 us (10%)
  local copies, waits for them, and re-layouts  5.76 us (5%)
  between operations  4.19 us (4%)
    ppermute x5, waiting for transfers between devices, shifted(): return lax.ppermute(x, axis, [(i, (i + by) % peers) for i in range(peers)])  23.9 us
    ppermute x3, starting transfers between devices, swapped(): return (lax.ppermute(inner, axis, within), outer)  21 us
    ppermute x5, starting transfers between devices, shifted(): return lax.ppermute(x, axis, [(i, (i + by) % peers) for i in range(peers)])  20.4 us
    pallas_call x7, Pallas kernels, call(): pl.pallas_call(kernel, out_shape=[jax.ShapeDtypeStruct(shape, jnp.float32...  9.87 us
    ppermute x3, starting transfers between devices, swapped(): outer = lax.ppermute(outer, axis, [(i, j % peers) for i, j in across])  6.55 us
    ppermute x1, waiting for transfers between devices, swapped(): lax.ppermute(outer, axis, [(i, j) for i, j in across if 0 <= j < peers])  6.2 us
    ppermute x1, starting transfers between devices, swapped(): inner = lax.ppermute(inner, axis, within)  4.36 us
    unnamed x11, local copies, waits for them, and re-layouts  3.36 us
  transfers between devices with their start and end apart: 13, of which 8 were waited for; matrix products, arithmetic and copies ran while one was open for 0% of the time, Pallas kernels for 0%

profile of v3, /device:TPU:33, one launch (start us, length us, event | category | flops | bytes accessed | tf_op | source)
XLA Modules:
  0.0 109.7 jit_solution(18236518122902128322)
XLA Ops:
  0.6 1.3 %fusion = (s32[1]{0:T(128)}, s32[1]{0:T(128)}) fusion(s32[2]{0:T(128)} %offsets.7), kind=kLoop, calls=%fused_computation.64 | loop fusion | bytes 16 | tf_op jit(solution)/shard_map/slice | solution.py:323
  3.6 16.3 %conditional.4 = (f32[3,8,16,128]{3,2,1,0:T(8,128)}) conditional(s32[]{:T(128)} %clamp.13, f32[3,8,16,128]{3,2,1,0:T(8,128)S(1)} %slice.397, f32[3,8,16,128]{3,2,1,0:T(8,128)S(1)} %slice.397, f32[3,8,16,128]{3,2,1,0:T(8,128)S(1)} %slice.397, f32[3,8,16,128]{3,2,1,0:T(8,128)S(1)} %slice.397, ...), branch_computations={%region_0.1_spmd, %region_1.2_spmd, %region_2.3_spmd, %region_3.4_... | conditional | bytes 786480 | solution.py:51
  3.6 4.0 %collective-permute-start.2 = (f32[3,8,16,128]{3,2,1,0:T(8,128)S(1)}, f32[3,8,16,128]{3,2,1,0:T(8,128)}, u32[]{:S(2)}, u32[]{:S(2)}) collective-permute-start(f32[3,8,16,128]{3,2,1,0:T(8,128)S(1)} %param.2), channel_id=1, source_target_pairs={{0,32},{16,48},{32,64},{48,80},{64,96},{80,112},{96,128},{112,144}... | collective-permute-start | bytes 589832 | tf_op jit(solution)/shard_map/cond/branch_2_fun/ppermute | solution.py:41
  7.6 12.3 %collective-permute-done.2 = f32[3,8,16,128]{3,2,1,0:T(8,128)} collective-permute-done((f32[3,8,16,128]{3,2,1,0:T(8,128)S(1)}, f32[3,8,16,128]{3,2,1,0:T(8,128)}, u32[]{:S(2)}, u32[]{:S(2)}) %collective-permute-start.2) | collective-permute-done | bytes 196640 | tf_op jit(solution)/shard_map/cond/branch_2_fun/ppermute | solution.py:41
  21.8 1.4 %shard_map.68 = (f32[3,8,8,256]{3,2,1,0:T(8,128)S(1)}, f32[3,8,8,256]{3,2,1,0:T(8,128)S(1)}, f32[3,8,16,128]{3,2,1,0:T(8,128)S(1)}, f32[3,8,16,256]{3,2,1,0:T(8,128)S(1)}, s32[8,16,256]{2,1,0:T(8,128)S(1)}) custom-call(f32[3,8,16,128]{3,2,1,0:T(8,128)} %get-tuple-element.376.rotor, f32[3,8,16,256]{3,2,1,0:T(8,128)S(1)} %copy-done, ...), custom_call_target="tpu_custom_call" | custom-call | tf_op jit(solution)/shard_map/pallas_call | solution.py:302
  23.3 4.4 %collective-permute-start.224 = (f32[3,8,8,256]{3,2,1,0:T(8,128)S(1)}, f32[3,8,8,256]{3,2,1,0:T(8,128)S(1)}, u32[]{:S(2)}, u32[]{:S(2)}) collective-permute-start(f32[3,8,8,256]{3,2,1,0:T(8,128)S(1)} %get-tuple-element.350), channel_id=1, source_target_pairs={{0,1},{1,0},{2,3},{3,2},{4,5},{5,4},{6,7},{7,6},{8,9},{9,8},{10,11... | collective-permute-start | bytes 589832 | tf_op jit(solution)/shard_map/ppermute | solution.py:80
  27.6 2.3 %collective-permute-start.225 = (f32[3,8,8,256]{3,2,1,0:T(8,128)S(1)}, f32[3,8,8,256]{3,2,1,0:T(8,128)S(1)}, u32[]{:S(2)}, u32[]{:S(2)}) collective-permute-start(f32[3,8,8,256]{3,2,1,0:T(8,128)S(1)} %get-tuple-element.351), channel_id=1, source_target_pairs={{1,2},{2,1},{3,4},{4,3},{5,6},{6,5},{7,8},{8,7},{9,10},{10,9},{11,... | collective-permute-start | bytes 589832 | tf_op jit(solution)/shard_map/ppermute | solution.py:81
  30.0 1.9 %collective-permute-done.224.inner = f32[3,8,8,256]{3,2,1,0:T(8,128)S(1)} collective-permute-done((f32[3,8,8,256]{3,2,1,0:T(8,128)S(1)}, f32[3,8,8,256]{3,2,1,0:T(8,128)S(1)}, u32[]{:S(2)}, u32[]{:S(2)}) %collective-permute-start.224) | collective-permute-done | bytes 196640 | tf_op jit(solution)/shard_map/ppermute | solution.py:80
  31.8 6.2 %collective-permute-done.225.outer = f32[3,8,8,256]{3,2,1,0:T(8,128)S(1)} collective-permute-done((f32[3,8,8,256]{3,2,1,0:T(8,128)S(1)}, f32[3,8,8,256]{3,2,1,0:T(8,128)S(1)}, u32[]{:S(2)}, u32[]{:S(2)}) %collective-permute-start.225) | collective-permute-done | bytes 196640 | tf_op jit(solution)/shard_map/ppermute | solution.py:81
  38.0 1.1 shard_map.69
  39.1 1.9 %collective-permute-start.226 = (f32[3,10,24,128]{3,2,1,0:T(8,128)S(1)}, f32[3,10,24,128]{3,2,1,0:T(8,128)S(1)}, u32[]{:S(2)}, u32[]{:S(2)}) collective-permute-start(f32[3,10,24,128]{3,2,1,0:T(8,128)S(1)} %get-tuple-element.355), channel_id=1, source_target_pairs={{0,496},{16,32},{32,16},{48,64},{64,48},{80,96},{96,80},{112,128},... | collective-permute-start | bytes 1105928 | tf_op jit(solution)/shard_map/ppermute | solution.py:78
  41.0 4.3 %collective-permute-start.227 = (f32[3,10,24,128]{3,2,1,0:T(8,128)S(1)}, f32[3,10,24,128]{3,2,1,0:T(8,128)S(1)}, u32[]{:S(2)}, u32[]{:S(2)}) collective-permute-start(f32[3,10,24,128]{3,2,1,0:T(8,128)S(1)} %get-tuple-element.356), channel_id=1, source_target_pairs={{0,16},{16,0},{32,48},{48,32},{64,80},{80,64},{96,112},{112,96},{1... | collective-permute-start | bytes 1105928 | tf_op jit(solution)/shard_map/ppermute | solution.py:79
  47.0 1.2 %collective-permute-done.226.outer.first_out = f32[3,10,24,128]{3,2,1,0:T(8,128)S(1)} collective-permute-done((f32[3,10,24,128]{3,2,1,0:T(8,128)S(1)}, f32[3,10,24,128]{3,2,1,0:T(8,128)S(1)}, u32[]{:S(2)}, u32[]{:S(2)}) %collective-permute-start.226) | collective-permute-done | bytes 368672 | tf_op jit(solution)/shard_map/ppermute | solution.py:78
  48.9 1.6 %shard_map.70 = (f32[10,24,256]{2,1,0:T(8,128)S(1)}, f32[3,8,24,128]{3,2,1,0:T(8,128)S(1)}, f32[3,8,24,128]{3,2,1,0:T(8,128)S(1)}) custom-call(s32[2]{0:T(128)S(1)} %copy-done.3, f32[3,10,24,128]{3,2,1,0:T(8,128)S(1)} %collective-permute-done.226.outer.first_out, f32[3,10,24,128]{3,2,1,0:T(8,128)S(1)} %collective-permute-done.227.inner.first_in, ...), custom_call_target="tpu_custom_call" | custom-call | tf_op jit(solution)/shard_map/pallas_call | solution.py:29
  50.5 7.4 %conditional.5 = (f32[3,8,24,128]{3,2,1,0:T(8,128)}) conditional(s32[]{:T(128)} %clamp.12, f32[3,8,24,128]{3,2,1,0:T(8,128)S(1)} %get-tuple-element.360, f32[3,8,24,128]{3,2,1,0:T(8,128)S(1)} %get-tuple-element.360, f32[3,8,24,128]{3,2,1,0:T(8,128)S(1)} %get-tuple-element.360, ...), branch_computations={%region_32.33_spmd, %region_33.34_spmd, %region_34.35_spmd, %regio... | conditional | bytes 1179696 | solution.py:51
  50.5 1.9 %collective-permute-start.33 = (f32[3,8,24,128]{3,2,1,0:T(8,128)S(1)}, f32[3,8,24,128]{3,2,1,0:T(8,128)}, u32[]{:S(2)}, u32[]{:S(2)}) collective-permute-start(f32[3,8,24,128]{3,2,1,0:T(8,128)S(1)} %param.33), channel_id=1, source_target_pairs={{0,16},{16,32},{32,48},{48,64},{64,80},{80,96},{96,112},{112,128},... | collective-permute-start | bytes 884744 | tf_op jit(solution)/shard_map/cond/branch_1_fun/ppermute | solution.py:41
  52.4 5.4 %collective-permute-done.33 = f32[3,8,24,128]{3,2,1,0:T(8,128)} collective-permute-done((f32[3,8,24,128]{3,2,1,0:T(8,128)S(1)}, f32[3,8,24,128]{3,2,1,0:T(8,128)}, u32[]{:S(2)}, u32[]{:S(2)}) %collective-permute-start.33) | collective-permute-done | bytes 294944 | tf_op jit(solution)/shard_map/cond/branch_1_fun/ppermute | solution.py:41
  57.9 1.0 shard_map.71
  58.9 2.7 %collective-permute-start.228 = (f32[3,8,24,128]{3,2,1,0:T(8,128)S(1)}, f32[3,8,24,128]{3,2,1,0:T(8,128)S(1)}, u32[]{:S(2)}, u32[]{:S(2)}) collective-permute-start(f32[3,8,24,128]{3,2,1,0:T(8,128)S(1)} %get-tuple-element.362), channel_id=1, source_target_pairs={{0,496},{16,32},{32,16},{48,64},{64,48},{80,96},{96,80},{112,128},... | collective-permute-start | bytes 884744 | tf_op jit(solution)/shard_map/ppermute | solution.py:78
  61.6 8.3 %collective-permute-start.229 = (f32[3,8,24,128]{3,2,1,0:T(8,128)S(1)}, f32[3,8,24,128]{3,2,1,0:T(8,128)S(1)}, u32[]{:S(2)}, u32[]{:S(2)}) collective-permute-start(f32[3,8,24,128]{3,2,1,0:T(8,128)S(1)} %get-tuple-element.363), channel_id=1, source_target_pairs={{0,16},{16,0},{32,48},{48,32},{64,80},{80,64},{96,112},{112,96},{1... | collective-permute-start | bytes 884744 | tf_op jit(solution)/shard_map/ppermute | solution.py:79
  71.0 2.9 %shard_map.72 = (f32[3,8,16,256]{3,2,1,0:T(8,128)}, f32[3,9,16,128]{3,2,1,0:T(8,128)S(1)}, f32[3,8,24,128]{3,2,1,0:T(8,128)S(1)}) custom-call(s32[2]{0:T(128)S(1)} %copy-done.3, f32[3,8,24,128]{3,2,1,0:T(8,128)S(1)} %collective-permute-done.228.outer, f32[3,8,24,128]{3,2,1,0:T(8,128)S(1)} %collective-permute-done.229.inner, ...), custom_call_target="tpu_custom_call" | custom-call | tf_op jit(solution)/shard_map/pallas_call | solution.py:29
  73.9 8.2 %conditional.6 = (f32[3,9,16,128]{3,2,1,0:T(8,128)}) conditional(s32[]{:T(128)} %clamp.15, f32[3,9,16,128]{3,2,1,0:T(8,128)S(1)} %get-tuple-element.366, f32[3,9,16,128]{3,2,1,0:T(8,128)S(1)} %get-tuple-element.366, f32[3,9,16,128]{3,2,1,0:T(8,128)S(1)} %get-tuple-element.366, ...), branch_computations={%region_64.65_spmd, %region_65.66_spmd, %region_66.67_spmd, %regio... | conditional | bytes 884784 | solution.py:51
  73.9 7.0 %collective-permute-start.95 = (f32[3,9,16,128]{3,2,1,0:T(8,128)S(1)}, f32[3,9,16,128]{3,2,1,0:T(8,128)}, u32[]{:S(2)}, u32[]{:S(2)}) collective-permute-start(f32[3,9,16,128]{3,2,1,0:T(8,128)S(1)} %param.95), channel_id=1, source_target_pairs={{0,496},{16,0},{32,16},{48,32},{64,48},{80,64},{96,80},{112,96},{1... | collective-permute-start | bytes 663560 | tf_op jit(solution)/shard_map/cond/branch_31_fun/ppermute | solution.py:41
  80.9 1.2 %collective-permute-done.95 = f32[3,9,16,128]{3,2,1,0:T(8,128)} collective-permute-done((f32[3,9,16,128]{3,2,1,0:T(8,128)S(1)}, f32[3,9,16,128]{3,2,1,0:T(8,128)}, u32[]{:S(2)}, u32[]{:S(2)}) %collective-permute-start.95) | collective-permute-done | bytes 221216 | tf_op jit(solution)/shard_map/cond/branch_31_fun/ppermute | solution.py:41
  83.1 1.9 %collective-permute-start.230 = (f32[3,6,24,128]{3,2,1,0:T(8,128)S(1)}, f32[3,6,24,128]{3,2,1,0:T(8,128)S(1)}, u32[]{:S(2)}, u32[]{:S(2)}) collective-permute-start(f32[3,6,24,128]{3,2,1,0:T(8,128)S(1)} %get-tuple-element.368), channel_id=1, source_target_pairs={{0,496},{16,32},{32,16},{48,64},{64,48},{80,96},{96,80},{112,128},... | collective-permute-start | bytes 663560 | tf_op jit(solution)/shard_map/ppermute | solution.py:78
  85.1 8.4 %collective-permute-start.231 = (f32[3,6,24,128]{3,2,1,0:T(8,128)S(1)}, f32[3,6,24,128]{3,2,1,0:T(8,128)S(1)}, u32[]{:S(2)}, u32[]{:S(2)}) collective-permute-start(f32[3,6,24,128]{3,2,1,0:T(8,128)S(1)} %get-tuple-element.369), channel_id=1, source_target_pairs={{0,16},{16,0},{32,48},{48,32},{64,80},{80,64},{96,112},{112,96},{1... | collective-permute-start | bytes 663560 | tf_op jit(solution)/shard_map/ppermute | solution.py:79
  94.9 1.1 shard_map.74
  95.9 12.5 %conditional.7 = (f32[3,11,16,128]{3,2,1,0:T(8,128)S(1)}) conditional(s32[]{:T(128)} %clamp.14, f32[3,8,16,128]{3,2,1,0:T(8,128)S(1)} %get-tuple-element.372, f32[3,8,16,128]{3,2,1,0:T(8,128)S(1)} %get-tuple-element.372, f32[3,8,16,128]{3,2,1,0:T(8,128)S(1)} %get-tuple-element.372, ...), branch_computations={%region_96.97_spmd, %region_97.98_spmd, %region_98.99_spmd, %regio... | conditional | flops 67584 | bytes 2162776 | solution.py:70
  96.0 5.5 %collective-permute-start.214 = (f32[3,7,16,128]{3,2,1,0:T(8,128)S(1)}, f32[3,7,16,128]{3,2,1,0:T(8,128)S(1)}, u32[]{:S(2)}, u32[]{:S(2)}) collective-permute-start(f32[3,7,16,128]{3,2,1,0:T(8,128)S(1)} %slice.384), channel_id=1, source_target_pairs={{0,480},{16,496},{32,0},{48,16},{64,32},{80,48},{96,64},{112,80},{... | collective-permute-start | bytes 516104 | tf_op jit(solution)/shard_map/cond/branch_59_fun/ppermute | solution.py:41
  101.5 1.9 %collective-permute-start.215 = (f32[3,4,16,128]{3,2,1,0:T(8,128)S(1)}, f32[3,4,16,128]{3,2,1,0:T(8,128)S(1)}, u32[]{:S(2)}, u32[]{:S(2)}) collective-permute-start(f32[3,4,16,128]{3,2,1,0:T(8,128)S(1)} %slice.385), channel_id=1, source_target_pairs={{0,464},{16,480},{32,496},{48,0},{64,16},{80,32},{96,48},{112,64},... | collective-permute-start | bytes 294920 | tf_op jit(solution)/shard_map/cond/branch_59_fun/ppermute | solution.py:41
  103.5 4.9 %collective-permute-done.215 = f32[3,4,16,128]{3,2,1,0:T(8,128)S(1)} collective-permute-done((f32[3,4,16,128]{3,2,1,0:T(8,128)S(1)}, f32[3,4,16,128]{3,2,1,0:T(8,128)S(1)}, u32[]{:S(2)}, u32[]{:S(2)}) %collective-permute-start.215) | collective-permute-done | bytes 98336 | tf_op jit(solution)/shard_map/cond/branch_59_fun/ppermute | solution.py:41
  108.4 1.3 %shard_map.75 = f32[3,8,16,256]{3,2,1,0:T(8,128)} custom-call(s32[2]{0:T(128)S(1)} %copy-done.3, f32[3,11,16,128]{3,2,1,0:T(8,128)S(1)} %get-tuple-element.379.rows, f32[3,8,16,128]{3,2,1,0:T(8,128)S(1)} %get-tuple-element.373.stator), custom_call_target="tpu_custom_call" | custom-call | tf_op jit(solution)/shard_map/pallas_call | solution.py:29
  (24 shorter events, 5.9 us)
Async XLA Ops:
  0.6 19.3 %copy-start = (f32[3,8,16,256]{3,2,1,0:T(8,128)S(1)}, f32[3,8,16,256]{3,2,1,0:T(8,128)}, u32[]{:S(2)}) copy-start(f32[3,8,16,256]{3,2,1,0:T(8,128)} %velocity.1) | copy-start | bytes 1179652
  3.6 16.3 %collective-permute-start.2 = (f32[3,8,16,128]{3,2,1,0:T(8,128)S(1)}, f32[3,8,16,128]{3,2,1,0:T(8,128)}, u32[]{:S(2)}, u32[]{:S(2)}) collective-permute-start(f32[3,8,16,128]{3,2,1,0:T(8,128)S(1)} %param.2), channel_id=1, source_target_pairs={{0,32},{16,48},{32,64},{48,80},{64,96},{80,112},{96,128},{112,144}... | collective-permute-start | bytes 589832 | tf_op jit(solution)/shard_map/cond/branch_2_fun/ppermute | solution.py:41
  19.9 1.0 copy-start.1
  20.9 0.9 copy-start.2
  23.3 8.6 %collective-permute-start.224 = (f32[3,8,8,256]{3,2,1,0:T(8,128)S(1)}, f32[3,8,8,256]{3,2,1,0:T(8,128)S(1)}, u32[]{:S(2)}, u32[]{:S(2)}) collective-permute-start(f32[3,8,8,256]{3,2,1,0:T(8,128)S(1)} %get-tuple-element.350), channel_id=1, source_target_pairs={{0,1},{1,0},{2,3},{3,2},{4,5},{5,4},{6,7},{7,6},{8,9},{9,8},{10,11... | collective-permute-start | bytes 589832 | tf_op jit(solution)/shard_map/ppermute | solution.py:80
  27.6 10.4 %collective-permute-start.225 = (f32[3,8,8,256]{3,2,1,0:T(8,128)S(1)}, f32[3,8,8,256]{3,2,1,0:T(8,128)S(1)}, u32[]{:S(2)}, u32[]{:S(2)}) collective-permute-start(f32[3,8,8,256]{3,2,1,0:T(8,128)S(1)} %get-tuple-element.351), channel_id=1, source_target_pairs={{1,2},{2,1},{3,4},{4,3},{5,6},{6,5},{7,8},{8,7},{9,10},{10,9},{11,... | collective-permute-start | bytes 589832 | tf_op jit(solution)/shard_map/ppermute | solution.py:81
  39.1 9.1 %collective-permute-start.226 = (f32[3,10,24,128]{3,2,1,0:T(8,128)S(1)}, f32[3,10,24,128]{3,2,1,0:T(8,128)S(1)}, u32[]{:S(2)}, u32[]{:S(2)}) collective-permute-start(f32[3,10,24,128]{3,2,1,0:T(8,128)S(1)} %get-tuple-element.355), channel_id=1, source_target_pairs={{0,496},{16,32},{32,16},{48,64},{64,48},{80,96},{96,80},{112,128},... | collective-permute-start | bytes 1105928 | tf_op jit(solution)/shard_map/ppermute | solution.py:78
  41.0 7.2 %collective-permute-start.227 = (f32[3,10,24,128]{3,2,1,0:T(8,128)S(1)}, f32[3,10,24,128]{3,2,1,0:T(8,128)S(1)}, u32[]{:S(2)}, u32[]{:S(2)}) collective-permute-start(f32[3,10,24,128]{3,2,1,0:T(8,128)S(1)} %get-tuple-element.356), channel_id=1, source_target_pairs={{0,16},{16,0},{32,48},{48,32},{64,80},{80,64},{96,112},{112,96},{1... | collective-permute-start | bytes 1105928 | tf_op jit(solution)/shard_map/ppermute | solution.py:79
  46.1 0.7 copy-start.4
  48.2 0.7 copy-start.3
  50.5 7.4 %collective-permute-start.33 = (f32[3,8,24,128]{3,2,1,0:T(8,128)S(1)}, f32[3,8,24,128]{3,2,1,0:T(8,128)}, u32[]{:S(2)}, u32[]{:S(2)}) collective-permute-start(f32[3,8,24,128]{3,2,1,0:T(8,128)S(1)} %param.33), channel_id=1, source_target_pairs={{0,16},{16,32},{32,48},{48,64},{64,80},{80,96},{96,112},{112,128},... | collective-permute-start | bytes 884744 | tf_op jit(solution)/shard_map/cond/branch_1_fun/ppermute | solution.py:41
  58.9 11.7 %collective-permute-start.228 = (f32[3,8,24,128]{3,2,1,0:T(8,128)S(1)}, f32[3,8,24,128]{3,2,1,0:T(8,128)S(1)}, u32[]{:S(2)}, u32[]{:S(2)}) collective-permute-start(f32[3,8,24,128]{3,2,1,0:T(8,128)S(1)} %get-tuple-element.362), channel_id=1, source_target_pairs={{0,496},{16,32},{32,16},{48,64},{64,48},{80,96},{96,80},{112,128},... | collective-permute-start | bytes 884744 | tf_op jit(solution)/shard_map/ppermute | solution.py:78
  61.6 9.5 %collective-permute-start.229 = (f32[3,8,24,128]{3,2,1,0:T(8,128)S(1)}, f32[3,8,24,128]{3,2,1,0:T(8,128)S(1)}, u32[]{:S(2)}, u32[]{:S(2)}) collective-permute-start(f32[3,8,24,128]{3,2,1,0:T(8,128)S(1)} %get-tuple-element.363), channel_id=1, source_target_pairs={{0,16},{16,0},{32,48},{48,32},{64,80},{80,64},{96,112},{112,96},{1... | collective-permute-start | bytes 884744 | tf_op jit(solution)/shard_map/ppermute | solution.py:79
  73.9 8.2 %collective-permute-start.95 = (f32[3,9,16,128]{3,2,1,0:T(8,128)S(1)}, f32[3,9,16,128]{3,2,1,0:T(8,128)}, u32[]{:S(2)}, u32[]{:S(2)}) collective-permute-start(f32[3,9,16,128]{3,2,1,0:T(8,128)S(1)} %param.95), channel_id=1, source_target_pairs={{0,496},{16,0},{32,16},{48,32},{64,48},{80,64},{96,80},{112,96},{1... | collective-permute-start | bytes 663560 | tf_op jit(solution)/shard_map/cond/branch_31_fun/ppermute | solution.py:41
  83.1 11.7 %collective-permute-start.230 = (f32[3,6,24,128]{3,2,1,0:T(8,128)S(1)}, f32[3,6,24,128]{3,2,1,0:T(8,128)S(1)}, u32[]{:S(2)}, u32[]{:S(2)}) collective-permute-start(f32[3,6,24,128]{3,2,1,0:T(8,128)S(1)} %get-tuple-element.368), channel_id=1, source_target_pairs={{0,496},{16,32},{32,16},{48,64},{64,48},{80,96},{96,80},{112,128},... | collective-permute-start | bytes 663560 | tf_op jit(solution)/shard_map/ppermute | solution.py:78
  85.1 9.8 %collective-permute-start.231 = (f32[3,6,24,128]{3,2,1,0:T(8,128)S(1)}, f32[3,6,24,128]{3,2,1,0:T(8,128)S(1)}, u32[]{:S(2)}, u32[]{:S(2)}) collective-permute-start(f32[3,6,24,128]{3,2,1,0:T(8,128)S(1)} %get-tuple-element.369), channel_id=1, source_target_pairs={{0,16},{16,0},{32,48},{48,32},{64,80},{80,64},{96,112},{112,96},{1... | collective-permute-start | bytes 663560 | tf_op jit(solution)/shard_map/ppermute | solution.py:79
  96.0 12.4 %collective-permute-start.214 = (f32[3,7,16,128]{3,2,1,0:T(8,128)S(1)}, f32[3,7,16,128]{3,2,1,0:T(8,128)S(1)}, u32[]{:S(2)}, u32[]{:S(2)}) collective-permute-start(f32[3,7,16,128]{3,2,1,0:T(8,128)S(1)} %slice.384), channel_id=1, source_target_pairs={{0,480},{16,496},{32,0},{48,16},{64,32},{80,48},{96,64},{112,80},{... | collective-permute-start | bytes 516104 | tf_op jit(solution)/shard_map/cond/branch_59_fun/ppermute | solution.py:41
  101.5 6.8 %collective-permute-start.215 = (f32[3,4,16,128]{3,2,1,0:T(8,128)S(1)}, f32[3,4,16,128]{3,2,1,0:T(8,128)S(1)}, u32[]{:S(2)}, u32[]{:S(2)}) collective-permute-start(f32[3,4,16,128]{3,2,1,0:T(8,128)S(1)} %slice.385), channel_id=1, source_target_pairs={{0,464},{16,480},{32,496},{48,0},{64,16},{80,32},{96,48},{112,64},... | collective-permute-start | bytes 294920 | tf_op jit(solution)/shard_map/cond/branch_59_fun/ppermute | solution.py:41

commit v4 on v3

--- a/solution.py
+++ b/solution.py
@@ -151,7 +151,15 @@
     send_rows(2, rotor_out, stator_out, seed_out, rows_in, rows_out)
 
 
-def pack_rows(rotor, stator, outer, inner):
+def pack_rows(packed, stator, outer, inner, rotor):
+    width = rotor.shape[1]
+    nz = packed.shape[2]
+    none = jnp.zeros((2, RB), jnp.float32)
+    for c in range(3):
+        for row in range(width):
+            rotor[c, row, :nz, :] = packed[c, row]
+            one, two, three = [packed[c, width + more, 2 * row : 2 * row + 2, :] for more in range(3)]
+            rotor[c, row, nz:, :] = jnp.concatenate([one, two[:1], none, two[1:], three], axis=0)
     send_rows(2, rotor, stator, None, inner, outer)
 
 
@@ -217,6 +225,7 @@
     for c in range(3):
         w[c] = multiply(w[c], weight)
     width, layers = rotor.shape[1:3]
+    nz = layers - 2 * ZH
     inside = within_ends(layers)
     for row in range(width + 2):
         sides = [around(w.at[c], row + 1) for c in range(3)]
@@ -226,8 +235,13 @@
             damp = 0.5 * solid[row - 1]
             for c in range(3):
                 u = inside * (sides[c][0] + 0.1 * mu * laplace(*sides[c]) - damp * sides[c][0])
-                u_rotor[c, row - 1] = u[:, :RB]
                 u_stator[c, row - 1] = u[:, RB:]
+                u_rotor[c, row - 1] = u[:nz, :RB]
+                at = 2 * row - 2
+                beyond = ((nz, nz + 1), (nz + 2, layers - 3), (layers - 2, layers - 1))
+                for more, pair in enumerate(beyond):
+                    for one, z in enumerate(pair):
+                        u_rotor[c, width + more, at + one : at + one + 1, :] = u[z : z + 1, :RB]
 
 
 def forward_last(
@@ -340,13 +354,13 @@
     first_in, first_out = swapped(inner, outer, "theta", True)
     visc, rotor, stator = call(
         forward_first,
-        [(width + 2, zs, NR), block, block],
+        [(width + 2, zs, NR), (3, width + 3, nz, RB), block],
         rotor_offset, first_out, first_in, rotor, stator, solid, spread,
         scratch=[ext(2 * width + 4), (3, width + 4, zs, NR)],
     )
 
     rotor = to_block(rotor, blocks1)
-    outer, inner = call(pack_rows, [ext(group + 4)] * 2, None, rotor, stator)
+    outer, inner, rotor = call(pack_rows, [ext(group + 4)] * 2 + [block], None, rotor, stator)
     inner, outer = swapped(inner, outer, "theta", True)
     ending, rotor, stator = call(
         forward_last,

time: 110 us -> 146 us (1.33); the launches traced: 110 us -> 144 us
  waiting for transfers between devices: 33.7 us -> 59.3 us
  starting transfers between devices: 54.6 us -> 63.5 us
    ppermute x5, waiting for transfers between devices: 23.9 us -> 47 us  [shifted(): return lax.ppermute(x, axis, [(i, (i + by) % peers) for i in range(peers)])]
    ppermute x3, starting transfers between devices: 21 us -> 7.15 us  [swapped(): return (lax.ppermute(inner, axis, within), outer)]
    ppermute x3, starting transfers between devices: 6.55 us -> 19.1 us  [swapped(): outer = lax.ppermute(outer, axis, [(i, j % peers) for i, j in across])]
    ppermute x5, starting transfers between devices: 20.4 us -> 30.5 us  [shifted(): return lax.ppermute(x, axis, [(i, (i + by) % peers) for i in range(peers)])]
    ppermute x3, waiting for transfers between devices: 1.25 us -> 4.33 us  [swapped(): outer = lax.ppermute(outer, axis, [(i, j % peers) for i, j in across])]
  transfers between devices with their start and end apart: 13 -> 13, of which waited for: 8 -> 9; matrix products, arithmetic and copies ran while one was open for 0% -> 0% of each run, Pallas kernels for 0% -> 0%
where the time goes in v4:
time: 146 us; the launch traced here: 144 us
  starting transfers between devices  63.5 us (43%)
  waiting for transfers between devices  59.3 us (41%)
  Pallas kernels  11.4 us (8%)
  local copies, waits for them, and re-layouts  5.75 us (4%)
  between operations  3.91 us (3%)
    ppermute x5, waiting for transfers between devices, shifted(): return lax.ppermute(x, axis, [(i, (i + by) % peers) for i in range(peers)])  47 us
    ppermute x5, starting transfers between devices, shifted(): return lax.ppermute(x, axis, [(i, (i + by) % peers) for i in range(peers)])  30.5 us
    ppermute x3, starting transfers between devices, swapped(): outer = lax.ppermute(outer, axis, [(i, j % peers) for i, j in across])  19.1 us
    pallas_call x7, Pallas kernels, call(): pl.pallas_call(kernel, out_shape=[jax.ShapeDtypeStruct(shape, jnp.float32...  9.95 us
    ppermute x3, starting transfers between devices, swapped(): return (lax.ppermute(inner, axis, within), outer)  7.15 us
    ppermute x1, waiting for transfers between devices, swapped(): lax.ppermute(outer, axis, [(i, j) for i, j in across if 0 <= j < peers])  5.08 us
    ppermute x1, starting transfers between devices, swapped(): inner = lax.ppermute(inner, axis, within)  4.65 us
    ppermute x3, waiting for transfers between devices, swapped(): outer = lax.ppermute(outer, axis, [(i, j % peers) for i, j in across])  4.33 us
  transfers between devices with their start and end apart: 13, of which 9 were waited for; matrix products, arithmetic and copies ran while one was open for 0% of the time, Pallas kernels for 0%

profile of v4, /device:TPU:33, one launch (start us, length us, event | category | flops | bytes accessed | tf_op | source)
XLA Modules:
  0.0 144.0 jit_solution(4522774802195918843)
XLA Ops:
  0.6 1.3 fusion
  3.5 22.3 %conditional.4 = (f32[3,8,16,128]{3,2,1,0:T(8,128)}) conditional(s32[]{:T(128)} %clamp.13, f32[3,8,16,128]{3,2,1,0:T(8,128)S(1)} %slice.397, f32[3,8,16,128]{3,2,1,0:T(8,128)S(1)} %slice.397, f32[3,8,16,128]{3,2,1,0:T(8,128)S(1)} %slice.397, f32[3,8,16,128]{3,2,1,0:T(8,128)S(1)} %slice.397, ...), branch_computations={%region_0.1_spmd, %region_1.2_spmd, %region_2.3_spmd, %region_3.4_... | conditional | bytes 786480 | solution.py:51
  3.5 11.2 %collective-permute-start.9 = (f32[3,8,16,128]{3,2,1,0:T(8,128)S(1)}, f32[3,8,16,128]{3,2,1,0:T(8,128)}, u32[]{:S(2)}, u32[]{:S(2)}) collective-permute-start(f32[3,8,16,128]{3,2,1,0:T(8,128)S(1)} %param.9), channel_id=1, source_target_pairs={{0,144},{16,160},{32,176},{48,192},{64,208},{80,224},{96,240},{112... | collective-permute-start | bytes 589832 | tf_op jit(solution)/shard_map/cond/branch_9_fun/ppermute | solution.py:41
  14.7 11.0 %collective-permute-done.9 = f32[3,8,16,128]{3,2,1,0:T(8,128)} collective-permute-done((f32[3,8,16,128]{3,2,1,0:T(8,128)S(1)}, f32[3,8,16,128]{3,2,1,0:T(8,128)}, u32[]{:S(2)}, u32[]{:S(2)}) %collective-permute-start.9) | collective-permute-done | bytes 196640 | tf_op jit(solution)/shard_map/cond/branch_9_fun/ppermute | solution.py:41
  27.7 1.4 shard_map.68
  29.1 4.7 %collective-permute-start.224 = (f32[3,8,8,256]{3,2,1,0:T(8,128)S(1)}, f32[3,8,8,256]{3,2,1,0:T(8,128)S(1)}, u32[]{:S(2)}, u32[]{:S(2)}) collective-permute-start(f32[3,8,8,256]{3,2,1,0:T(8,128)S(1)} %get-tuple-element.351), channel_id=1, source_target_pairs={{0,1},{1,0},{2,3},{3,2},{4,5},{5,4},{6,7},{7,6},{8,9},{9,8},{10,11... | collective-permute-start | bytes 589832 | tf_op jit(solution)/shard_map/ppermute | solution.py:80
  33.8 2.0 %collective-permute-start.225 = (f32[3,8,8,256]{3,2,1,0:T(8,128)S(1)}, f32[3,8,8,256]{3,2,1,0:T(8,128)S(1)}, u32[]{:S(2)}, u32[]{:S(2)}) collective-permute-start(f32[3,8,8,256]{3,2,1,0:T(8,128)S(1)} %get-tuple-element.352), channel_id=1, source_target_pairs={{1,2},{2,1},{3,4},{4,3},{5,6},{6,5},{7,8},{8,7},{9,10},{10,9},{11,... | collective-permute-start | bytes 589832 | tf_op jit(solution)/shard_map/ppermute | solution.py:81
  35.8 2.9 %collective-permute-done.224.inner = f32[3,8,8,256]{3,2,1,0:T(8,128)S(1)} collective-permute-done((f32[3,8,8,256]{3,2,1,0:T(8,128)S(1)}, f32[3,8,8,256]{3,2,1,0:T(8,128)S(1)}, u32[]{:S(2)}, u32[]{:S(2)}) %collective-permute-start.224) | collective-permute-done | bytes 196640 | tf_op jit(solution)/shard_map/ppermute | solution.py:80
  38.7 5.1 %collective-permute-done.225.outer = f32[3,8,8,256]{3,2,1,0:T(8,128)S(1)} collective-permute-done((f32[3,8,8,256]{3,2,1,0:T(8,128)S(1)}, f32[3,8,8,256]{3,2,1,0:T(8,128)S(1)}, u32[]{:S(2)}, u32[]{:S(2)}) %collective-permute-start.225) | collective-permute-done | bytes 196640 | tf_op jit(solution)/shard_map/ppermute | solution.py:81
  43.8 1.1 shard_map.69
  44.9 3.2 %collective-permute-start.226 = (f32[3,10,24,128]{3,2,1,0:T(8,128)S(1)}, f32[3,10,24,128]{3,2,1,0:T(8,128)S(1)}, u32[]{:S(2)}, u32[]{:S(2)}) collective-permute-start(f32[3,10,24,128]{3,2,1,0:T(8,128)S(1)} %get-tuple-element.356), channel_id=1, source_target_pairs={{0,496},{16,32},{32,16},{48,64},{64,48},{80,96},{96,80},{112,128},... | collective-permute-start | bytes 1105928 | tf_op jit(solution)/shard_map/ppermute | solution.py:78
  48.1 2.0 %collective-permute-start.227 = (f32[3,10,24,128]{3,2,1,0:T(8,128)S(1)}, f32[3,10,24,128]{3,2,1,0:T(8,128)S(1)}, u32[]{:S(2)}, u32[]{:S(2)}) collective-permute-start(f32[3,10,24,128]{3,2,1,0:T(8,128)S(1)} %get-tuple-element.357), channel_id=1, source_target_pairs={{0,16},{16,0},{32,48},{48,32},{64,80},{80,64},{96,112},{112,96},{1... | collective-permute-start | bytes 1105928 | tf_op jit(solution)/shard_map/ppermute | solution.py:79
  51.6 2.1 %collective-permute-done.226.outer.first_out = f32[3,10,24,128]{3,2,1,0:T(8,128)S(1)} collective-permute-done((f32[3,10,24,128]{3,2,1,0:T(8,128)S(1)}, f32[3,10,24,128]{3,2,1,0:T(8,128)S(1)}, u32[]{:S(2)}, u32[]{:S(2)}) %collective-permute-start.226) | collective-permute-done | bytes 368672 | tf_op jit(solution)/shard_map/ppermute | solution.py:78
  54.4 1.6 %shard_map.70 = (f32[10,24,256]{2,1,0:T(8,128)S(1)}, f32[3,11,16,128]{3,2,1,0:T(8,128)S(1)}, f32[3,8,24,128]{3,2,1,0:T(8,128)S(1)}) custom-call(s32[2]{0:T(128)S(1)} %copy-done.3, f32[3,10,24,128]{3,2,1,0:T(8,128)S(1)} %collective-permute-done.226.outer.first_out, f32[3,10,24,128]{3,2,1,0:T(8,128)S(1)} %collective-permute-done.227.inner.first_in, ...), custom_call_target="tpu_custom_call" | custom-call | tf_op jit(solution)/shard_map/pallas_call | solution.py:29
  55.9 23.3 %conditional.5 = (f32[3,11,16,128]{3,2,1,0:T(8,128)}) conditional(s32[]{:T(128)} %clamp.12, f32[3,11,16,128]{3,2,1,0:T(8,128)S(1)} %get-tuple-element.361, f32[3,11,16,128]{3,2,1,0:T(8,128)S(1)} %get-tuple-element.361, f32[3,11,16,128]{3,2,1,0:T(8,128)S(1)} %get-tuple-element.361, ...), branch_computations={%region_32.33_spmd, %region_33.34_spmd, %region_34.35_spmd, %regio... | conditional | bytes 1081392 | solution.py:51
  56.0 5.5 %collective-permute-start.38 = (f32[3,11,16,128]{3,2,1,0:T(8,128)S(1)}, f32[3,11,16,128]{3,2,1,0:T(8,128)}, u32[]{:S(2)}, u32[]{:S(2)}) collective-permute-start(f32[3,11,16,128]{3,2,1,0:T(8,128)S(1)} %param.38), channel_id=1, source_target_pairs={{0,96},{16,112},{32,128},{48,144},{64,160},{80,176},{96,192},{112,... | collective-permute-start | bytes 811016 | tf_op jit(solution)/shard_map/cond/branch_6_fun/ppermute | solution.py:41
  61.4 17.8 %collective-permute-done.38 = f32[3,11,16,128]{3,2,1,0:T(8,128)} collective-permute-done((f32[3,11,16,128]{3,2,1,0:T(8,128)S(1)}, f32[3,11,16,128]{3,2,1,0:T(8,128)}, u32[]{:S(2)}, u32[]{:S(2)}) %collective-permute-start.38) | collective-permute-done | bytes 270368 | tf_op jit(solution)/shard_map/cond/branch_6_fun/ppermute | solution.py:41
  79.2 1.7 %shard_map.71 = (f32[3,8,24,128]{3,2,1,0:T(8,128)}, f32[3,8,24,128]{3,2,1,0:T(8,128)S(1)}, f32[3,8,24,128]{3,2,1,0:T(8,128)S(1)}) custom-call(f32[3,11,16,128]{3,2,1,0:T(8,128)} %get-tuple-element.379.packed, f32[3,8,24,128]{3,2,1,0:T(8,128)S(1)} %get-tuple-element.362.stator), custom_call_target="tpu_custom_call" | custom-call | tf_op jit(solution)/shard_map/pallas_call | solution.py:29
  81.0 6.0 %collective-permute-start.228 = (f32[3,8,24,128]{3,2,1,0:T(8,128)}, f32[3,8,24,128]{3,2,1,0:T(8,128)S(1)}, u32[]{:S(2)}, u32[]{:S(2)}) collective-permute-start(f32[3,8,24,128]{3,2,1,0:T(8,128)} %get-tuple-element.363), channel_id=1, source_target_pairs={{0,496},{16,32},{32,16},{48,64},{64,48},{80,96},{96,80},{112,128},... | collective-permute-start | bytes 884744 | tf_op jit(solution)/shard_map/ppermute | solution.py:78
  87.0 1.9 %collective-permute-start.229 = (f32[3,8,24,128]{3,2,1,0:T(8,128)S(1)}, f32[3,8,24,128]{3,2,1,0:T(8,128)S(1)}, u32[]{:S(2)}, u32[]{:S(2)}) collective-permute-start(f32[3,8,24,128]{3,2,1,0:T(8,128)S(1)} %get-tuple-element.364), channel_id=1, source_target_pairs={{0,16},{16,0},{32,48},{48,32},{64,80},{80,64},{96,112},{112,96},{1... | collective-permute-start | bytes 884744 | tf_op jit(solution)/shard_map/ppermute | solution.py:79
  89.7 2.3 %collective-permute-done.228.outer = f32[3,8,24,128]{3,2,1,0:T(8,128)S(1)} collective-permute-done((f32[3,8,24,128]{3,2,1,0:T(8,128)}, f32[3,8,24,128]{3,2,1,0:T(8,128)S(1)}, u32[]{:S(2)}, u32[]{:S(2)}) %collective-permute-start.228) | collective-permute-done | bytes 294944 | tf_op jit(solution)/shard_map/ppermute | solution.py:78
  91.9 2.2 %shard_map.72 = (f32[3,8,16,256]{3,2,1,0:T(8,128)}, f32[3,9,16,128]{3,2,1,0:T(8,128)S(1)}, f32[3,8,24,128]{3,2,1,0:T(8,128)S(1)}) custom-call(s32[2]{0:T(128)S(1)} %copy-done.3, f32[3,8,24,128]{3,2,1,0:T(8,128)S(1)} %collective-permute-done.228.outer, f32[3,8,24,128]{3,2,1,0:T(8,128)S(1)} %collective-permute-done.229.inner, ...), custom_call_target="tpu_custom_call" | custom-call | tf_op jit(solution)/shard_map/pallas_call | solution.py:29
  94.1 13.5 %conditional.6 = (f32[3,9,16,128]{3,2,1,0:T(8,128)}) conditional(s32[]{:T(128)} %clamp.15, f32[3,9,16,128]{3,2,1,0:T(8,128)S(1)} %get-tuple-element.368, f32[3,9,16,128]{3,2,1,0:T(8,128)S(1)} %get-tuple-element.368, f32[3,9,16,128]{3,2,1,0:T(8,128)S(1)} %get-tuple-element.368, ...), branch_computations={%region_64.65_spmd, %region_65.66_spmd, %region_66.67_spmd, %regio... | conditional | bytes 884784 | solution.py:51
  94.1 3.6 %collective-permute-start.90 = (f32[3,9,16,128]{3,2,1,0:T(8,128)S(1)}, f32[3,9,16,128]{3,2,1,0:T(8,128)}, u32[]{:S(2)}, u32[]{:S(2)}) collective-permute-start(f32[3,9,16,128]{3,2,1,0:T(8,128)S(1)} %param.90), channel_id=1, source_target_pairs={{0,416},{16,432},{32,448},{48,464},{64,480},{80,496},{96,0},{112,1... | collective-permute-start | bytes 663560 | tf_op jit(solution)/shard_map/cond/branch_26_fun/ppermute | solution.py:41
  97.7 9.9 %collective-permute-done.90 = f32[3,9,16,128]{3,2,1,0:T(8,128)} collective-permute-done((f32[3,9,16,128]{3,2,1,0:T(8,128)S(1)}, f32[3,9,16,128]{3,2,1,0:T(8,128)}, u32[]{:S(2)}, u32[]{:S(2)}) %collective-permute-start.90) | collective-permute-done | bytes 221216 | tf_op jit(solution)/shard_map/cond/branch_26_fun/ppermute | solution.py:41
  108.7 9.9 %collective-permute-start.230 = (f32[3,6,24,128]{3,2,1,0:T(8,128)S(1)}, f32[3,6,24,128]{3,2,1,0:T(8,128)S(1)}, u32[]{:S(2)}, u32[]{:S(2)}) collective-permute-start(f32[3,6,24,128]{3,2,1,0:T(8,128)S(1)} %get-tuple-element.370), channel_id=1, source_target_pairs={{0,496},{16,32},{32,16},{48,64},{64,48},{80,96},{96,80},{112,128},... | collective-permute-start | bytes 663560 | tf_op jit(solution)/shard_map/ppermute | solution.py:78
  118.6 3.3 %collective-permute-start.231 = (f32[3,6,24,128]{3,2,1,0:T(8,128)S(1)}, f32[3,6,24,128]{3,2,1,0:T(8,128)S(1)}, u32[]{:S(2)}, u32[]{:S(2)}) collective-permute-start(f32[3,6,24,128]{3,2,1,0:T(8,128)S(1)} %get-tuple-element.371), channel_id=1, source_target_pairs={{0,16},{16,0},{32,48},{48,32},{64,80},{80,64},{96,112},{112,96},{1... | collective-permute-start | bytes 663560 | tf_op jit(solution)/shard_map/ppermute | solution.py:79
  124.1 18.6 %conditional.7 = (f32[3,11,16,128]{3,2,1,0:T(8,128)S(1)}) conditional(s32[]{:T(128)} %clamp.14, f32[3,8,16,128]{3,2,1,0:T(8,128)S(1)} %get-tuple-element.374, f32[3,8,16,128]{3,2,1,0:T(8,128)S(1)} %get-tuple-element.374, f32[3,8,16,128]{3,2,1,0:T(8,128)S(1)} %get-tuple-element.374, ...), branch_computations={%region_96.97_spmd, %region_97.98_spmd, %region_98.99_spmd, %regio... | conditional | flops 67584 | bytes 2162776 | solution.py:70
  124.2 3.4 %collective-permute-start.186 = (f32[3,7,16,128]{3,2,1,0:T(8,128)S(1)}, f32[3,7,16,128]{3,2,1,0:T(8,128)S(1)}, u32[]{:S(2)}, u32[]{:S(2)}) collective-permute-start(f32[3,7,16,128]{3,2,1,0:T(8,128)S(1)} %slice.363), channel_id=1, source_target_pairs={{0,368},{16,384},{32,400},{48,416},{64,432},{80,448},{96,464},{112... | collective-permute-start | bytes 516104 | tf_op jit(solution)/shard_map/cond/branch_45_fun/ppermute | solution.py:41
  127.6 6.8 %collective-permute-start.187 = (f32[3,4,16,128]{3,2,1,0:T(8,128)S(1)}, f32[3,4,16,128]{3,2,1,0:T(8,128)S(1)}, u32[]{:S(2)}, u32[]{:S(2)}) collective-permute-start(f32[3,4,16,128]{3,2,1,0:T(8,128)S(1)} %slice.364), channel_id=1, source_target_pairs={{0,352},{16,368},{32,384},{48,400},{64,416},{80,432},{96,448},{112... | collective-permute-start | bytes 294920 | tf_op jit(solution)/shard_map/cond/branch_45_fun/ppermute | solution.py:41
  134.4 8.2 %collective-permute-done.187 = f32[3,4,16,128]{3,2,1,0:T(8,128)S(1)} collective-permute-done((f32[3,4,16,128]{3,2,1,0:T(8,128)S(1)}, f32[3,4,16,128]{3,2,1,0:T(8,128)S(1)}, u32[]{:S(2)}, u32[]{:S(2)}) %collective-permute-start.187) | collective-permute-done | bytes 98336 | tf_op jit(solution)/shard_map/cond/branch_45_fun/ppermute | solution.py:41
  142.7 1.3 shard_map.75
  (24 shorter events, 6.6 us)
Async XLA Ops:
  0.6 25.1 %copy-start = (f32[3,8,16,256]{3,2,1,0:T(8,128)S(1)}, f32[3,8,16,256]{3,2,1,0:T(8,128)}, u32[]{:S(2)}) copy-start(f32[3,8,16,256]{3,2,1,0:T(8,128)} %velocity.1) | copy-start | bytes 1179652
  3.5 22.2 %collective-permute-start.9 = (f32[3,8,16,128]{3,2,1,0:T(8,128)S(1)}, f32[3,8,16,128]{3,2,1,0:T(8,128)}, u32[]{:S(2)}, u32[]{:S(2)}) collective-permute-start(f32[3,8,16,128]{3,2,1,0:T(8,128)S(1)} %param.9), channel_id=1, source_target_pairs={{0,144},{16,160},{32,176},{48,192},{64,208},{80,224},{96,240},{112... | collective-permute-start | bytes 589832 | tf_op jit(solution)/shard_map/cond/branch_9_fun/ppermute | solution.py:41
  25.8 1.0 copy-start.1
  26.8 0.9 copy-start.2
  29.1 9.6 %collective-permute-start.224 = (f32[3,8,8,256]{3,2,1,0:T(8,128)S(1)}, f32[3,8,8,256]{3,2,1,0:T(8,128)S(1)}, u32[]{:S(2)}, u32[]{:S(2)}) collective-permute-start(f32[3,8,8,256]{3,2,1,0:T(8,128)S(1)} %get-tuple-element.351), channel_id=1, source_target_pairs={{0,1},{1,0},{2,3},{3,2},{4,5},{5,4},{6,7},{7,6},{8,9},{9,8},{10,11... | collective-permute-start | bytes 589832 | tf_op jit(solution)/shard_map/ppermute | solution.py:80
  33.8 10.0 %collective-permute-start.225 = (f32[3,8,8,256]{3,2,1,0:T(8,128)S(1)}, f32[3,8,8,256]{3,2,1,0:T(8,128)S(1)}, u32[]{:S(2)}, u32[]{:S(2)}) collective-permute-start(f32[3,8,8,256]{3,2,1,0:T(8,128)S(1)} %get-tuple-element.352), channel_id=1, source_target_pairs={{1,2},{2,1},{3,4},{4,3},{5,6},{6,5},{7,8},{8,7},{9,10},{10,9},{11,... | collective-permute-start | bytes 589832 | tf_op jit(solution)/shard_map/ppermute | solution.py:81
  44.9 8.8 %collective-permute-start.226 = (f32[3,10,24,128]{3,2,1,0:T(8,128)S(1)}, f32[3,10,24,128]{3,2,1,0:T(8,128)S(1)}, u32[]{:S(2)}, u32[]{:S(2)}) collective-permute-start(f32[3,10,24,128]{3,2,1,0:T(8,128)S(1)} %get-tuple-element.356), channel_id=1, source_target_pairs={{0,496},{16,32},{32,16},{48,64},{64,48},{80,96},{96,80},{112,128},... | collective-permute-start | bytes 1105928 | tf_op jit(solution)/shard_map/ppermute | solution.py:78
  48.1 5.6 %collective-permute-start.227 = (f32[3,10,24,128]{3,2,1,0:T(8,128)S(1)}, f32[3,10,24,128]{3,2,1,0:T(8,128)S(1)}, u32[]{:S(2)}, u32[]{:S(2)}) collective-permute-start(f32[3,10,24,128]{3,2,1,0:T(8,128)S(1)} %get-tuple-element.357), channel_id=1, source_target_pairs={{0,16},{16,0},{32,48},{48,32},{64,80},{80,64},{96,112},{112,96},{1... | collective-permute-start | bytes 1105928 | tf_op jit(solution)/shard_map/ppermute | solution.py:79
  50.7 0.7 copy-start.4
  53.7 0.7 copy-start.3
  56.0 23.3 %collective-permute-start.38 = (f32[3,11,16,128]{3,2,1,0:T(8,128)S(1)}, f32[3,11,16,128]{3,2,1,0:T(8,128)}, u32[]{:S(2)}, u32[]{:S(2)}) collective-permute-start(f32[3,11,16,128]{3,2,1,0:T(8,128)S(1)} %param.38), channel_id=1, source_target_pairs={{0,96},{16,112},{32,128},{48,144},{64,160},{80,176},{96,192},{112,... | collective-permute-start | bytes 811016 | tf_op jit(solution)/shard_map/cond/branch_6_fun/ppermute | solution.py:41
  81.0 10.9 %collective-permute-start.228 = (f32[3,8,24,128]{3,2,1,0:T(8,128)}, f32[3,8,24,128]{3,2,1,0:T(8,128)S(1)}, u32[]{:S(2)}, u32[]{:S(2)}) collective-permute-start(f32[3,8,24,128]{3,2,1,0:T(8,128)} %get-tuple-element.363), channel_id=1, source_target_pairs={{0,496},{16,32},{32,16},{48,64},{64,48},{80,96},{96,80},{112,128},... | collective-permute-start | bytes 884744 | tf_op jit(solution)/shard_map/ppermute | solution.py:78
  87.0 4.9 %collective-permute-start.229 = (f32[3,8,24,128]{3,2,1,0:T(8,128)S(1)}, f32[3,8,24,128]{3,2,1,0:T(8,128)S(1)}, u32[]{:S(2)}, u32[]{:S(2)}) collective-permute-start(f32[3,8,24,128]{3,2,1,0:T(8,128)S(1)} %get-tuple-element.364), channel_id=1, source_target_pairs={{0,16},{16,0},{32,48},{48,32},{64,80},{80,64},{96,112},{112,96},{1... | collective-permute-start | bytes 884744 | tf_op jit(solution)/shard_map/ppermute | solution.py:79
  94.1 13.5 %collective-permute-start.90 = (f32[3,9,16,128]{3,2,1,0:T(8,128)S(1)}, f32[3,9,16,128]{3,2,1,0:T(8,128)}, u32[]{:S(2)}, u32[]{:S(2)}) collective-permute-start(f32[3,9,16,128]{3,2,1,0:T(8,128)S(1)} %param.90), channel_id=1, source_target_pairs={{0,416},{16,432},{32,448},{48,464},{64,480},{80,496},{96,0},{112,1... | collective-permute-start | bytes 663560 | tf_op jit(solution)/shard_map/cond/branch_26_fun/ppermute | solution.py:41
  108.7 14.3 %collective-permute-start.230 = (f32[3,6,24,128]{3,2,1,0:T(8,128)S(1)}, f32[3,6,24,128]{3,2,1,0:T(8,128)S(1)}, u32[]{:S(2)}, u32[]{:S(2)}) collective-permute-start(f32[3,6,24,128]{3,2,1,0:T(8,128)S(1)} %get-tuple-element.370), channel_id=1, source_target_pairs={{0,496},{16,32},{32,16},{48,64},{64,48},{80,96},{96,80},{112,128},... | collective-permute-start | bytes 663560 | tf_op jit(solution)/shard_map/ppermute | solution.py:78
  118.6 4.4 %collective-permute-start.231 = (f32[3,6,24,128]{3,2,1,0:T(8,128)S(1)}, f32[3,6,24,128]{3,2,1,0:T(8,128)S(1)}, u32[]{:S(2)}, u32[]{:S(2)}) collective-permute-start(f32[3,6,24,128]{3,2,1,0:T(8,128)S(1)} %get-tuple-element.371), channel_id=1, source_target_pairs={{0,16},{16,0},{32,48},{48,32},{64,80},{80,64},{96,112},{112,96},{1... | collective-permute-start | bytes 663560 | tf_op jit(solution)/shard_map/ppermute | solution.py:79
  124.2 18.5 %collective-permute-start.186 = (f32[3,7,16,128]{3,2,1,0:T(8,128)S(1)}, f32[3,7,16,128]{3,2,1,0:T(8,128)S(1)}, u32[]{:S(2)}, u32[]{:S(2)}) collective-permute-start(f32[3,7,16,128]{3,2,1,0:T(8,128)S(1)} %slice.363), channel_id=1, source_target_pairs={{0,368},{16,384},{32,400},{48,416},{64,432},{80,448},{96,464},{112... | collective-permute-start | bytes 516104 | tf_op jit(solution)/shard_map/cond/branch_45_fun/ppermute | solution.py:41
  127.6 15.0 %collective-permute-start.187 = (f32[3,4,16,128]{3,2,1,0:T(8,128)S(1)}, f32[3,4,16,128]{3,2,1,0:T(8,128)S(1)}, u32[]{:S(2)}, u32[]{:S(2)}) collective-permute-start(f32[3,4,16,128]{3,2,1,0:T(8,128)S(1)} %slice.364), channel_id=1, source_target_pairs={{0,352},{16,368},{32,384},{48,400},{64,416},{80,432},{96,448},{112... | collective-permute-start | bytes 294920 | tf_op jit(solution)/shard_map/cond/branch_45_fun/ppermute | solution.py:41
